TPU v7x, 512 devices: a whole 4x4x16 slice. The times are simulated.
512 devices in a mesh: ctx: 32 (over y, z_lo, core), fsdp: 16 (over x, z_hi).
Axes of the slice: x: 4, y: 4, z: 16 (z_hi: 4, z_lo: 4; z = z_hi * 4 + z_lo), core: 2. Of those that a mesh axis runs over, the one named last changes fastest.
Arguments:
- query: bfloat16 [16384, 8192], P('ctx', 'fsdp'), may hold values from -6 to 6
- key_in: bfloat16 [16384, 8192], P('ctx', 'fsdp'), may hold values from -6 to 6
- value_in: bfloat16 [16384, 8192], P('ctx', 'fsdp'), may hold values from -6 to 6
- cotangent: bfloat16 [16384, 8192], P('ctx', 'fsdp'), may hold values from -6 to 6
- filter_weight: float32 [128, 512], P('fsdp', 'ctx'), may hold values from -0.5 to 0.5
- log_rate: float32 [512], P('ctx'), may hold values from -6 to -3
Outputs:
- output: bfloat16 [16384, 8192], P('ctx', 'fsdp')
- grad_query: bfloat16 [16384, 8192], P('ctx', 'fsdp')
- grad_key: bfloat16 [16384, 8192], P('ctx', 'fsdp')
- grad_value: bfloat16 [16384, 8192], P('ctx', 'fsdp')
- grad_filter: float32 [128, 512], P('fsdp', 'ctx')
- grad_log_rate: float32 [512], P('ctx')
All inputs are finite; a program needn't handle non-finite values.
Results may differ from a plain program's by a relative error of at most 0.0057.
Values may be sent and summed in bfloat16 or wider, within the bound.
No kernel may reach another device: no remote copies, remote signals or barrier semaphores. Data moves between devices by JAX's collectives and lax.ppermute only.
A program may use at most 64 MiB of HBM per device.

v0:
```python
import math

import jax
import jax.numpy as jnp
from jax import lax
from jax.sharding import PartitionSpec as P

FILT = 128
GROUP = 16


def passed_along(value, axis, by):
    peers = lax.axis_size(axis)
    pairs = [(i, i + by) for i in range(peers) if 0 <= i + by < peers]
    return lax.ppermute(value, axis, pairs)


def lag_table(rows_in, rows_out, forward):
    rows_a = lax.broadcasted_iota(jnp.int32, (rows_in, rows_out), 0)
    cols_b = lax.broadcasted_iota(jnp.int32, (rows_in, rows_out), 1)
    if forward:
        return cols_b + (rows_in - rows_out) - rows_a
    return rows_a - cols_b


def band_table(filt_len, lag_values):
    tap_ids = lax.broadcasted_iota(jnp.int32, (filt_len,) + lag_values.shape, 0)
    return (tap_ids == lag_values[None]).astype(jnp.bfloat16)


def banded(filters, onehot_table):
    return jnp.einsum(
        "jg,jat->gat", filters, onehot_table, preferred_element_type=jnp.float32
    ).astype(jnp.bfloat16)


def to_groups(row_major):
    return row_major.T.reshape(row_major.shape[1] // GROUP, GROUP, row_major.shape[0])


def from_groups(grouped):
    return grouped.reshape(-1, grouped.shape[-1]).T


def apply_band(pair_blocks, kernel):
    return jnp.einsum("gkba,gat->gkbt", pair_blocks, kernel, preferred_element_type=jnp.float32)


def filter_terms(pair_blocks, grad_blocks, onehot_table):
    outer_sums = jnp.einsum(
        "gkba,gkbt->gat", pair_blocks, grad_blocks, preferred_element_type=jnp.float32
    )
    return jnp.einsum(
        "gat,jat->jg", outer_sums, onehot_table.astype(jnp.float32), precision=lax.Precision.HIGHEST
    )


def per_device(query, key_in, value_in, cotangent, filter_weight, log_rate):
    token_count = query.shape[0]
    channel_count = query.shape[1]
    filt_len = FILT
    halo_rows = filt_len - 1
    tokens_all = token_count * lax.axis_size("ctx")
    grad_scale = 1.0 / math.sqrt(tokens_all * GROUP)
    group_count = channel_count // GROUP
    group_start = lax.axis_index("fsdp") * group_count
    weights_ctx, rates_all = (
        lax.all_gather(filter_weight, "ctx", axis=1, tiled=True),
        lax.all_gather(log_rate, "ctx", axis=0, tiled=True),
    )
    all_taps = lax.all_gather(weights_ctx, "fsdp", axis=0, tiled=True)
    tap_weights = lax.dynamic_slice_in_dim(all_taps, group_start, group_count, 1)
    own_log = lax.dynamic_slice_in_dim(rates_all, group_start, group_count, 0)
    tap_index = jnp.arange(filt_len, dtype=jnp.float32)[:, None]
    filters = (tap_weights * jnp.exp(-jnp.exp(own_log)[None, :] * tap_index)).astype(jnp.bfloat16)
    products = (key_in.astype(jnp.float32) * value_in.astype(jnp.float32)).astype(jnp.bfloat16)
    block_count = token_count // filt_len
    earlier = passed_along(products[token_count - halo_rows :], "ctx", 1)
    zero_row = jnp.zeros((1, channel_count), jnp.bfloat16)
    grouped = to_groups(jnp.concatenate([zero_row, earlier, products], axis=0))
    grouped = grouped.reshape(group_count, GROUP, block_count + 1, filt_len)
    pair_blocks = jnp.concatenate([grouped[:, :, :-1], grouped[:, :, 1:]], axis=3)
    forward_table = band_table(filt_len, lag_table(2 * filt_len, filt_len, True))
    back_table = band_table(filt_len, lag_table(2 * filt_len, filt_len, False))
    mixed_blocks = apply_band(pair_blocks, banded(filters, forward_table))
    mixed_rows = from_groups(mixed_blocks.reshape(group_count, GROUP, token_count))
    query_wide = query.astype(jnp.float32)
    cotangent_wide = cotangent.astype(jnp.float32)
    output = (query_wide * mixed_rows).astype(jnp.bfloat16)
    grad_mixed = (cotangent_wide * query_wide).astype(jnp.bfloat16)
    grad_query = (cotangent_wide * mixed_rows).astype(jnp.bfloat16)
    later_pieces = passed_along(grad_mixed[:halo_rows], "ctx", -1)
    grad_grouped = to_groups(jnp.concatenate([grad_mixed, later_pieces, zero_row], axis=0))
    grad_grouped = grad_grouped.reshape(group_count, GROUP, block_count + 1, filt_len)
    grad_blocks = jnp.concatenate([grad_grouped[:, :, :-1], grad_grouped[:, :, 1:]], axis=3)
    grad_prod_blocks = apply_band(grad_blocks, banded(filters, back_table))
    grad_products = from_groups(grad_prod_blocks.reshape(group_count, GROUP, token_count))
    grad_key = (grad_products * value_in.astype(jnp.float32)).astype(jnp.bfloat16)
    grad_value = (grad_products * key_in.astype(jnp.float32)).astype(jnp.bfloat16)
    partial_sums = filter_terms(pair_blocks, grad_grouped[:, :, :-1], forward_table)
    groups_all = all_taps.shape[1]
    embedded = lax.dynamic_update_slice(
        jnp.zeros((filt_len, groups_all), jnp.float32), partial_sums, (jnp.int32(0), group_start)
    )
    tap_count = filter_weight.shape[0]
    tap_part = lax.psum_scatter(embedded, "fsdp", scatter_dimension=0, tiled=True)
    own_sums = lax.psum_scatter(tap_part, "ctx", scatter_dimension=1, tiled=True)
    first_tap = lax.axis_index("fsdp") * tap_count
    own_taps = (first_tap + lax.broadcasted_iota(jnp.int32, (tap_count, 1), 0)).astype(jnp.float32)
    decay_rates = jnp.exp(log_rate)
    own_decays = jnp.exp(-decay_rates[None, :] * own_taps)
    grad_filter = own_sums * own_decays * grad_scale
    rate_terms = jnp.sum(
        own_sums * filter_weight * own_decays * (-own_taps * decay_rates[None, :]), axis=0
    )
    grad_log_rate = lax.psum(rate_terms, "fsdp") * grad_scale
    return (output, grad_query, grad_key, grad_value, grad_filter, grad_log_rate)


def solution(mesh):
    return jax.shard_map(
        per_device,
        mesh=mesh,
        in_specs=(
            P("ctx", "fsdp"),
            P("ctx", "fsdp"),
            P("ctx", "fsdp"),
            P("ctx", "fsdp"),
            P("fsdp", "ctx"),
            P("ctx"),
        ),
        out_specs=(
            P("ctx", "fsdp"),
            P("ctx", "fsdp"),
            P("ctx", "fsdp"),
            P("ctx", "fsdp"),
            P("fsdp", "ctx"),
            P("ctx"),
        ),
        check_vma=False,
    )
```

profile of v0, /device:TPU:128, one launch (start us, length us, event | category | flops | bytes accessed | tf_op | source)
XLA Modules:
  0.0 524.1 jit_solution(856138307177335165)
XLA Ops:
  7.2 1.3 copy.70
  8.5 1.3 copy.79
  10.0 1.3 collective-permute-start.1
  12.0 1.3 dynamic-slice
  14.1 75.8 %all-reduce = f32[512]{0:T(512)S(1)} all-reduce(f32[512]{0:T(512)S(1)} %dynamic-update-slice), channel_id=1, replica_groups=mesh['ctx'=32,'fsdp'=16] {'ctx'}, use_global_device_ids=true, to_apply=%add | all-reduce | flops 512 | bytes 4096
  89.9 38.1 %all-gather = f32[32,16,8]{1,2,0:T(8,128)S(1)} all-gather(f32[1,16,8]{1,2,0:T(8,128)S(1)} %bitcast.60), channel_id=1, replica_groups=mesh['ctx'=32,'fsdp'=16] {'ctx'}, dimensions={0}, use_global_device_ids=true | all-gather | bytes 16896 | tf_op jit(solution)/shard_map/all_gather | solution.py:68
  128.2 51.8 %all_gather.10 = f32[128,512]{1,0:T(8,128)S(1)} all-gather(f32[8,512]{1,0:T(8,128)S(1)} %bitcast.59), channel_id=1, replica_groups=mesh['ctx'=32,'fsdp'=16] {'fsdp'}, dimensions={0}, use_global_device_ids=true | all-gather | bytes 278528 | tf_op jit(solution)/shard_map/all_gather | solution.py:71
  180.2 1.0 copy.71
  182.2 5.2 convert_bitcast_fusion
  187.4 1.0 maximum_bitcast_fusion.1
  189.8 1.2 copy-done.16
  191.0 1.3 fusion.7
  193.5 1.1 fusion.15
  194.8 1.5 collective-permute-start
  200.1 9.2 %fusion.11 = f32[128,32]{1,0:T(8,128)S(1)} fusion(f32[32,256,128]{2,1,0:T(8,128)S(1)} %convolution_bitcast_fusion, s32[256,128]{1,0:T(8,128)S(1)} %iota_subtract_fusion.1), kind=kOutput, calls=%fused_computation.22 | convolution fusion | flops 1614807040 | bytes 4341760 | tf_op jit(solution)/shard_map/gat,jat->jg/dot_general | solution.py:53
  209.3 1.1 dynamic_update_slice.3
  211.1 5.8 %convert_bitcast_fusion.1 = bf16[32,256,128,1]{2,0,1,3:T(8,128)(2,1)} fusion(s32[256,128]{1,0:T(8,128)S(1)} %iota_subtract_fusion.1, f32[128,32]{0,1:T(8,128)S(1)} %copy.103, f32[32]{0:T(128)} %copy-done.15), kind=kOutput, calls=%fused_computation.15 | convolution fusion | flops 273690624 | bytes 2244736 | tf_op jit(solution)/shard_map/jg,jat->gat/dot_general | solution.py:32
  219.0 2.8 fusion.9
  222.2 95.1 %reduce-scatter.5.cloned.1.call-done = f32[8,512]{1,0:T(8,128)} async-done(((f32[128,512]{1,0:T(8,128)}), f32[8,512]{1,0:T(8,128)}) %reduce-scatter.5.cloned.1.call-update) | async-done | bytes 16400 | tf_op jit(solution)/shard_map/reduce_scatter | solution.py:106
  317.3 1.5 copy.99
  319.2 1.0 copy.86
  320.2 1.0 copy.87
  321.2 145.2 %reduce-scatter.7.cloned.1.call-done = f32[16,8]{1,0:T(8,128)} async-done(((f32[512,8]{1,0:T(8,128)}), f32[16,8]{1,0:T(8,128)}) %reduce-scatter.7.cloned.1.call-update) | async-done | bytes 528
  467.9 48.8 %psum.7 = f32[16]{0:T(128)S(1)} all-reduce(f32[16]{0:T(128)S(1)} %get-tuple-element.39), channel_id=1, replica_groups=mesh['ctx'=32,'fsdp'=16] {'fsdp'}, use_global_device_ids=true, to_apply=%region_3.0 | all-reduce | flops 16 | bytes 128 | tf_op jit(solution)/shard_map/psum | solution.py:116
  (76 shorter events, 14.3 us)
Async XLA Ops:
  7.2 4.2 copy-start.14
  7.2 82.7 %copy-start.8 = (f32[8,16]{1,0:T(8,128)S(1)}, f32[8,16]{1,0:T(8,128)}, u32[]{:S(2)}) copy-start(f32[8,16]{1,0:T(8,128)} %param.10) | copy-start | bytes 1540
  7.2 310.1 %reduce-scatter.5.cloned.1.call-start = ((), (), s32[]{:S(2)}) async-start(), calls=%async_computation.2 | async-start | bytes 278528 | tf_op jit(solution)/shard_map/reduce_scatter | solution.py:106
  8.5 171.7 %copy-start.6 = (bf16[512,512]{1,0:T(8,128)(2,1)S(1)}, bf16[512,512]{1,0:T(8,128)(2,1)}, u32[]{:S(2)}) copy-start(bf16[512,512]{1,0:T(8,128)(2,1)} %param.7) | copy-start | bytes 1572868
  9.8 171.4 %copy-start.7 = (bf16[512,512]{1,0:T(8,128)(2,1)S(1)}, bf16[512,512]{1,0:T(8,128)(2,1)}, u32[]{:S(2)}) copy-start(bf16[512,512]{1,0:T(8,128)(2,1)} %param.8) | copy-start | bytes 1572868
  10.0 177.4 %collective-permute-start.1 = (bf16[127,512]{0,1:T(8,128)(2,1)S(1)}, bf16[127,512]{0,1:T(8,128)(2,1)}, u32[]{:S(2)}, u32[]{:S(2)}) collective-permute-start(bf16[127,512]{0,1:T(8,128)(2,1)S(1)} %slice.28), channel_id=1, source_target_pairs={{16,0},{32,16},{48,32},{64,48},{80,64},{96,80},{112,96},{128,112},... | collective-permute-start | bytes 390152 | tf_op jit(solution)/shard_map/ppermute | solution.py:15
  180.0 7.4 %copy-start.15 = (f32[32]{0:T(128)}, f32[32]{0:T(128)S(1)}, u32[]{:S(2)}) copy-start(f32[32]{0:T(128)S(1)} %exponential_negate_fusion) | copy-start | bytes 388
  189.2 1.8 copy-start.16
  189.6 2.7 copy-start.3
  192.3 1.0 copy-start.1
  192.3 1.2 copy-start.2
  194.8 2.6 collective-permute-start
  198.3 1.0 copy-start.4
  210.3 0.7 copy-start.5
  210.4 6.6 %copy-start = (bf16[512,512]{0,1:T(8,128)(2,1)S(1)}, bf16[512,512]{0,1:T(8,128)(2,1)}, u32[]{:S(2)}) copy-start(bf16[512,512]{0,1:T(8,128)(2,1)} %get-tuple-element.31) | copy-start | bytes 1572868
  211.1 255.3 %reduce-scatter.7.cloned.1.call-start = ((), (), s32[]{:S(2)}) async-start(), calls=%async_computation.3 | async-start | bytes 270336
  318.9 148.3 %copy-start.9 = (f32[8,16]{1,0:T(8,128)S(1)}, f32[8,16]{1,0:T(8,128)}, u32[]{:S(2)}) copy-start(f32[8,16]{1,0:T(8,128)} %param.10) | copy-start | bytes 1540
  318.9 148.3 %copy-start.10 = (f32[16]{0:T(128)S(1)}, f32[16]{0:T(128)}, u32[]{:S(2)}) copy-start(f32[16]{0:T(128)} %get-tuple-element.41) | copy-start | bytes 196
  318.9 148.3 %copy-start.11 = (f32[16]{0:T(128)S(1)}, f32[16]{0:T(128)}, u32[]{:S(2)}) copy-start(f32[16]{0:T(128)} %get-tuple-element.42) | copy-start | bytes 196
  318.9 148.3 %copy-start.12 = (f32[8]{0:T(128)S(1)}, f32[8]{0:T(128)}, u32[]{:S(2)}) copy-start(f32[8]{0:T(128)} %add_convert_fusion) | copy-start | bytes 100
  318.9 148.2 %copy-start.13 = (f32[8]{0:T(128)S(1)}, f32[8]{0:T(128)}, u32[]{:S(2)}) copy-start(f32[8]{0:T(128)} %fusion.27) | copy-start | bytes 100
Sparse Core Ops, SparseCore 0:
  211.2 106.0 reduce-scatter.4
  320.3 146.0 reduce-scatter.6
where the time goes:
time: 525 us; the launch traced here: 524 us
  waiting for transfers between devices  240 us (46%)
  blocking collectives  215 us (41%)
  matrix products  25 us (5%)
  local copies, waits for them, and re-layouts  20.5 us (4%)
  between operations  15.1 us (3%)
  other arithmetic  5.74 us (1%)
    unnamed x3, waiting for transfers between devices  145 us
    reduce_scatter x1, waiting for transfers between devices, per_device(): lax.psum_scatter(embedded, 'fsdp', scatter_dimension=0, tiled=True)  95.1 us
    unnamed x1, blocking collectives  75.8 us
    all_gather x1, blocking collectives, per_device(): all_taps = lax.all_gather(weights_ctx, 'fsdp', axis=0, tiled=True)  51.8 us
    psum x1, blocking collectives, per_device(): grad_log_rate = lax.psum(rate_terms, 'fsdp') * grad_scale  48.8 us
    all_gather x1, blocking collectives, per_device(): lax.all_gather(filter_weight, 'ctx', axis=1, tiled=True)  38.1 us
    unnamed x52, local copies, waits for them, and re-layouts  15.7 us
    dot_general x2, matrix products, banded(): jnp.einsum('jg,jat->gat', filters, onehot_table, preferred_element_type=j...  11 us
  transfers between devices with their start and end apart: 4, of which 2 were waited for; matrix products, arithmetic and copies ran while one was open for 5% of the time, Pallas kernels for 0%

commit v1 on v0

v1 whole, which is shorter than its diff:
```python
import math

import jax
import jax.numpy as jnp
from jax import lax
from jax.experimental import pallas as pl
from jax.experimental.pallas import tpu as pltpu
from jax.sharding import PartitionSpec as P

FILT = 128
GROUP = 16
LANES = 128
F32 = jnp.float32
BF16 = jnp.bfloat16
VMEM_BYTES = 48 * 1024 * 1024
NT = (((1,), (1,)), ((), ()))


def iota(shape, dim):
    return lax.broadcasted_iota(jnp.int32, shape, dim)


def rounded_product(a, b):
    return (a.astype(F32) * b.astype(F32)).astype(BF16)


def edges_kernel(key_ref, value_ref, query_ref, cot_ref, weight_ref, rate_ref, tail_ref, head_ref, taps_ref):
    tail_ref[...] = rounded_product(key_ref[...], value_ref[...])
    head_ref[...] = rounded_product(cot_ref[...], query_ref[...])
    tap_count, group_count = weight_ref.shape
    first_tap = lax.axis_index("fsdp") * tap_count
    taps = (first_tap + iota((tap_count, group_count), 0)).astype(F32)
    decayed = weight_ref[...] * jnp.exp(-jnp.exp(rate_ref[...]) * taps)
    high = decayed.astype(BF16).astype(F32)
    taps_ref[...] = jnp.zeros_like(taps_ref)
    taps_ref[:, :group_count] = high
    taps_ref[:, group_count : 2 * group_count] = decayed - high


def sums_kernel(key_ref, value_ref, query_ref, cot_ref, next_ref, sums_ref):
    rows = key_ref.shape[0]
    blocks = rows // FILT
    products = rounded_product(key_ref[...], value_ref[...])
    grads = jnp.concatenate([rounded_product(cot_ref[...], query_ref[...]), next_ref[...]], axis=0)
    left = jnp.concatenate([products[b * FILT : (b + 1) * FILT] for b in range(blocks)], axis=1)
    right = jnp.concatenate([grads[b * FILT : (b + 2) * FILT] for b in range(blocks)], axis=1)
    groups = LANES // GROUP
    lane_group = (iota(left.shape, 1) % LANES) // GROUP
    zero = jnp.zeros_like(left)
    stacked = jnp.concatenate([jnp.where(lane_group == g, left, zero) for g in range(groups)], axis=0)
    outer = lax.dot_general(stacked, right, NT, preferred_element_type=F32)
    later = iota((FILT, FILT), 1) >= iota((FILT, FILT), 0)
    rolled = jnp.zeros((groups * 8, LANES), F32)
    merged = [
        jnp.where(later, outer[g * FILT : (g + 1) * FILT, :FILT], outer[g * FILT : (g + 1) * FILT, FILT:])
        for g in range(groups)
    ]
    for i in range(FILT // 8):
        part = jnp.concatenate([m[8 * i : 8 * i + 8] for m in merged], axis=0)
        rolled = rolled + (pltpu.roll(part, FILT - 8 * i, axis=1) if i else part)
    row = iota(rolled.shape, 0) % 8
    for step in (1, 2, 4):
        rolled = jnp.where((row & step) != 0, pltpu.roll(rolled, FILT - step, axis=1), rolled)
    sums_ref[...] = rolled.reshape(groups, 8, LANES).sum(axis=1)


def message_kernel(sums_ref, taps_ref, out_ref):
    half = sums_ref.shape[0] // 2
    taps = taps_ref[...]
    halves = [
        jnp.concatenate([sums_ref[h * half : (h + 1) * half], taps], axis=0).astype(BF16) for h in range(2)
    ]
    for peer in range(out_ref.shape[0]):
        out_ref[peer] = halves[peer % 2]


def reduce_kernel(recv_ref, filt_ref, flipped_ref, home_ref):
    peers, rows, _ = recv_ref.shape
    half = GROUP
    total = jnp.zeros((half, LANES), F32)
    pieces = ([], [])
    for peer in range(peers):
        message = recv_ref[peer].astype(F32)
        total = total + message[:half]
        pieces[peer % 2].append(message[half:])
    eye = (iota((2 * half, LANES), 0) == iota((2 * half, LANES), 1)).astype(F32)
    turned = [
        lax.dot_general(
            eye.astype(BF16), jnp.concatenate(p, axis=0).astype(BF16), NT, preferred_element_type=F32
        )
        for p in pieces
    ]
    high = jnp.concatenate([t[:half] for t in turned], axis=0)
    flip = ((iota((FILT, FILT), 0) + iota((FILT, FILT), 1)) % FILT == 0).astype(BF16)
    filt_ref[...] = high
    flipped_ref[...] = jnp.dot(high.astype(BF16), flip, preferred_element_type=F32)
    own = lax.axis_index("ctx")
    decayed = [t[:half] + t[half:] for t in turned]
    own_decayed = jnp.where(own % 2 == 0, decayed[0], decayed[1])
    lane = iota((half, LANES), 1)
    rate = jnp.sum(own_decayed * total * lane.astype(F32), axis=1, keepdims=True)
    tap_count = 8
    moved = pltpu.roll(total, (FILT - tap_count * (own // 2)) % FILT, axis=1)
    home_ref[...] = jnp.where(lane < tap_count, moved, rate)


def circulants(rows):
    return jnp.concatenate(
        [
            pltpu.roll(jnp.broadcast_to(rows[g : g + 1], (FILT, FILT)), 0, axis=1, stride=1, stride_axis=0)
            for g in range(rows.shape[0])
        ],
        axis=0,
    )


def banded_pair(rows, first, second):
    whole = circulants(rows)
    zero = jnp.zeros_like(whole)
    return jnp.concatenate([jnp.where(first, whole, zero), jnp.where(second, whole, zero)], axis=1).astype(BF16)


def apply_filters(band, padded, blocks):
    right = jnp.concatenate([padded[b * FILT : (b + 2) * FILT] for b in range(blocks)], axis=1)
    wide = jnp.dot(band, right, preferred_element_type=F32)
    lane_group = iota((FILT, LANES), 1) // GROUP
    out = []
    for b in range(blocks):
        kept = wide[:FILT, b * LANES : (b + 1) * LANES]
        for g in range(1, LANES // GROUP):
            kept = jnp.where(
                lane_group == g, wide[g * FILT : (g + 1) * FILT, b * LANES : (b + 1) * LANES], kept
            )
        out.append(kept)
    return out


def outputs_kernel(
    key_ref, value_ref, query_ref, cot_ref, before_ref, after_ref, filt_ref, flipped_ref,
    output_ref, grad_query_ref, grad_key_ref, grad_value_ref,
):
    blocks = key_ref.shape[0] // FILT
    groups = LANES // GROUP
    shape = (groups * FILT, FILT)
    row, col = iota(shape, 0) % FILT, iota(shape, 1)
    above, lower = row < col, row >= col
    key, value = key_ref[...].astype(F32), value_ref[...].astype(F32)
    query, cot = query_ref[...].astype(F32), cot_ref[...].astype(F32)
    products = jnp.concatenate([before_ref[...], (key * value).astype(BF16)], axis=0)
    forward = banded_pair(flipped_ref[...], above, lower)
    for b, mixed in enumerate(apply_filters(forward, products, blocks)):
        rows = slice(b * FILT, (b + 1) * FILT)
        output_ref[rows] = (query[rows] * mixed).astype(BF16)
        grad_query_ref[rows] = (cot[rows] * mixed).astype(BF16)
    grads = jnp.concatenate([(cot * query).astype(BF16), after_ref[...]], axis=0)
    backward = banded_pair(filt_ref[...], row <= col, row > col)
    for b, back in enumerate(apply_filters(backward, grads, blocks)):
        rows = slice(b * FILT, (b + 1) * FILT)
        grad_key_ref[rows] = (back * value[rows]).astype(BF16)
        grad_value_ref[rows] = (back * key[rows]).astype(BF16)


def finish_kernel(home_ref, rate_ref, grad_filter_ref, grad_rate_ref, *, scale):
    tap_count, group_count = grad_filter_ref.shape
    turned = home_ref[...].T
    first_tap = lax.axis_index("fsdp") * tap_count
    taps = (first_tap + iota((tap_count, group_count), 0)).astype(F32)
    rates = jnp.exp(rate_ref[...])
    grad_filter_ref[...] = turned[:tap_count, :group_count] * jnp.exp(-rates * taps) * scale
    grad_rate_ref[...] = turned[tap_count : tap_count + 1, :group_count] * (-rates) * scale


def params():
    return pltpu.CompilerParams(vmem_limit_bytes=VMEM_BYTES)


def swap_axes(value):
    ctx, fsdp = lax.axis_size("ctx"), lax.axis_size("fsdp")
    pairs = [(c * fsdp + f, (2 * f + c % 2) * fsdp + c // 2) for c in range(ctx) for f in range(fsdp)]
    return lax.ppermute(value, ("ctx", "fsdp"), pairs)


def passed_along(value, by):
    peers = lax.axis_size("ctx")
    pairs = [(i, i + by) for i in range(peers) if 0 <= i + by < peers]
    return lax.ppermute(value, "ctx", pairs)


def per_device(query, key_in, value_in, cotangent, filter_weight, log_rate):
    tokens, channels = query.shape
    peers = lax.axis_size("ctx")
    groups = channels // GROUP
    scale = 1.0 / math.sqrt(tokens * peers * GROUP)
    rate_row = log_rate.reshape(1, -1)
    sds = jax.ShapeDtypeStruct
    last = tokens // FILT - 1
    tap_count, tap_groups = filter_weight.shape

    tail_spec = pl.BlockSpec((FILT, channels), lambda i: (last, 0))
    head_spec = pl.BlockSpec((FILT, channels), lambda i: (0, 0))
    tail, head, taps = pl.pallas_call(
        edges_kernel,
        grid=(1,),
        in_specs=[
            tail_spec, tail_spec, head_spec, head_spec,
            pl.BlockSpec(filter_weight.shape, lambda i: (0, 0)),
            pl.BlockSpec(rate_row.shape, lambda i: (0, 0)),
        ],
        out_specs=[head_spec, head_spec, pl.BlockSpec((tap_count, LANES), lambda i: (0, 0))],
        out_shape=[
            sds((FILT, channels), BF16), sds((FILT, channels), BF16), sds((tap_count, LANES), F32),
        ],
        compiler_params=params(),
    )(key_in, value_in, query, cotangent, filter_weight, rate_row)
    after = passed_along(head, -1)
    taps_here = swap_axes(taps)
    before = passed_along(tail, 1)

    tile = pl.BlockSpec((tokens, LANES), lambda i: (0, i))
    halo = pl.BlockSpec((FILT, LANES), lambda i: (0, i))
    group_rows = pl.BlockSpec((LANES // GROUP, LANES), lambda i: (i, 0))
    sums = pl.pallas_call(
        sums_kernel,
        grid=(channels // LANES,),
        in_specs=[tile, tile, tile, tile, halo],
        out_specs=group_rows,
        out_shape=sds((groups, LANES), F32),
        compiler_params=params(),
    )(key_in, value_in, query, cotangent, after)
    message = pl.pallas_call(
        message_kernel,
        out_shape=sds((peers, groups // 2 + tap_count, LANES), BF16),
        compiler_params=params(),
    )(sums, taps_here)
    received = lax.all_to_all(message, "ctx", 0, 0, tiled=True)
    filt, flipped, home = pl.pallas_call(
        reduce_kernel,
        out_shape=[sds((groups, LANES), F32), sds((groups, LANES), F32), sds((groups // 2, LANES), F32)],
        compiler_params=params(),
    )(received)
    home = swap_axes(home)
    output, grad_query, grad_key, grad_value = pl.pallas_call(
        outputs_kernel,
        grid=(channels // LANES,),
        in_specs=[tile, tile, tile, tile, halo, halo, group_rows, group_rows],
        out_specs=[tile] * 4,
        out_shape=[sds((tokens, channels), BF16)] * 4,
        compiler_params=params(),
    )(key_in, value_in, query, cotangent, before, after, filt, flipped)
    grad_filter, grad_rate = pl.pallas_call(
        lambda *refs: finish_kernel(*refs, scale=scale),
        out_shape=[sds(filter_weight.shape, F32), sds(rate_row.shape, F32)],
        compiler_params=params(),
    )(home, rate_row)
    return (output, grad_query, grad_key, grad_value, grad_filter, grad_rate.reshape(log_rate.shape))


def solution(mesh):
    specs = (P("ctx", "fsdp"),) * 4 + (P("fsdp", "ctx"), P("ctx"))
    return jax.shard_map(per_device, mesh=mesh, in_specs=specs, out_specs=specs, check_vma=False)
```

time: 525 us -> 63.7 us (0.12)
  the two profiles are of different devices: /device:TPU:128 before, /device:TPU:73 now
where the time goes in v1:
time: 63.7 us; the launch traced here: 63.2 us
  starting transfers between devices  43.5 us (68%)
  Pallas kernels  9.79 us (15%)
  local copies, waits for them, and re-layouts  5.52 us (9%)
  waiting for transfers between devices  3.64 us (6%)
  between operations  0.77 us (1%)
    ppermute x2, starting transfers between devices, swap_axes(): return lax.ppermute(value, ('ctx', 'fsdp'), pairs)  29.6 us
    all_to_all x1, starting transfers between devices, per_device(): received = lax.all_to_all(message, 'ctx', 0, 0, tiled=True)  8.05 us
    ppermute x2, starting transfers between devices, passed_along(): return lax.ppermute(value, 'ctx', pairs)  5.92 us
    unnamed x20, local copies, waits for them, and re-layouts  5.52 us
    pallas_call x1, Pallas kernels, per_device(): pl.pallas_call(outputs_kernel, grid=(channels // LANES,), in_specs=[tile,...  4.59 us
    all_to_all x1, waiting for transfers between devices, per_device(): received = lax.all_to_all(message, 'ctx', 0, 0, tiled=True)  3.63 us
    pallas_call x1, Pallas kernels, per_device(): pl.pallas_call(sums_kernel, grid=(channels // LANES,), in_specs=[tile, ti...  3.48 us
  transfers between devices with their start and end apart: 5, of which 1 were waited for; matrix products, arithmetic and copies ran while one was open for 0% of the time, Pallas kernels for 13%

profile of v1, /device:TPU:73, one launch (start us, length us, event | category | flops | bytes accessed | tf_op | source)
XLA Modules:
  0.0 63.2 jit_solution(4600693832844056096)
XLA Ops:
  0.6 0.6 %copy-done.9 = f32[16]{0:T(128)S(1)} copy-done((f32[16]{0:T(128)S(1)}, f32[16]{0:T(128)}, u32[]{:S(2)}) %copy-start.9) | copy-done | bytes 88
  1.3 1.0 %copy-done = bf16[512,512]{1,0:T(8,128)(2,1)S(1)} copy-done((bf16[512,512]{1,0:T(8,128)(2,1)S(1)}, bf16[512,512]{1,0:T(8,128)(2,1)}, u32[]{:S(2)}) %copy-start) | copy-done | bytes 524312
  2.3 1.0 %copy-done.2 = bf16[512,512]{1,0:T(8,128)(2,1)S(1)} copy-done((bf16[512,512]{1,0:T(8,128)(2,1)S(1)}, bf16[512,512]{1,0:T(8,128)(2,1)}, u32[]{:S(2)}) %copy-start.2) | copy-done | bytes 524312
  3.4 1.0 %copy-done.4 = bf16[512,512]{1,0:T(8,128)(2,1)S(1)} copy-done((bf16[512,512]{1,0:T(8,128)(2,1)S(1)}, bf16[512,512]{1,0:T(8,128)(2,1)}, u32[]{:S(2)}) %copy-start.4) | copy-done | bytes 524312
  4.4 1.0 %copy-done.6 = bf16[512,512]{1,0:T(8,128)(2,1)S(1)} copy-done((bf16[512,512]{1,0:T(8,128)(2,1)S(1)}, bf16[512,512]{1,0:T(8,128)(2,1)}, u32[]{:S(2)}) %copy-start.6) | copy-done | bytes 524312
  5.5 0.7 %copy-done.8 = f32[8,16]{1,0:T(8,128)S(1)} copy-done((f32[8,16]{1,0:T(8,128)S(1)}, f32[8,16]{1,0:T(8,128)}, u32[]{:S(2)}) %copy-start.8) | copy-done | bytes 536
  6.1 0.2 shard_map.109
  6.3 2.6 %collective-permute-start.1 = (bf16[128,512]{1,0:T(8,128)(2,1)S(1)}, bf16[128,512]{1,0:T(8,128)(2,1)S(1)}, u32[]{:S(2)}, u32[]{:S(2)}) collective-permute-start(bf16[128,512]{1,0:T(8,128)(2,1)S(1)} %get-tuple-element.19), channel_id=1, source_target_pairs={{16,0},{32,16},{48,32},{64,48},{80,64},{96,80},{112,96},{128,112},... | collective-permute-start | bytes 393224 | tf_op jit(solution)/shard_map/ppermute | solution.py:186
  8.9 13.5 %collective-permute-start.2 = (f32[8,128]{1,0:T(8,128)S(1)}, f32[8,128]{1,0:T(8,128)S(1)}, u32[]{:S(2)}, u32[]{:S(2)}) collective-permute-start(f32[8,128]{1,0:T(8,128)S(1)} %get-tuple-element.20), channel_id=1, source_target_pairs={{0,0},{1,32},{2,64},{3,96},{4,128},{5,160},{6,192},{7,224},{8,256}... | collective-permute-start | bytes 12296 | tf_op jit(solution)/shard_map/ppermute | solution.py:180
  22.5 0.0 collective-permute-done.1.next_ref.after_ref
  22.5 0.0 copy-start.3
  22.5 0.0 copy-start.5
  22.5 0.0 copy-start.7
  22.5 3.5 %shard_map.110.sums_ref = f32[32,128]{1,0:T(8,128)S(1)} custom-call(bf16[512,512]{1,0:T(8,128)(2,1)S(1)} %copy-done, bf16[512,512]{1,0:T(8,128)(2,1)S(1)} %copy-done.2, bf16[512,512]{1,0:T(8,128)(2,1)S(1)} %copy-done.4, bf16[512,512]{1,0:T(8,128)(2,1)S(1)} %copy-done.6, bf16[128,512]{1,0:T(8,128)(2,1)S(1)} %collective-permute-done.1.next_ref.after_ref), custom_call_target="tpu_custom_call" | custom-call | tf_op jit(solution)/shard_map/pallas_call | solution.py:222
  26.0 0.7 %shard_map.111 = bf16[32,24,128]{2,1,0:T(8,128)(2,1)} custom-call(f32[32,128]{1,0:T(8,128)S(1)} %shard_map.110.sums_ref, f32[8,128]{1,0:T(8,128)S(1)} %collective-permute-done.2.taps_ref), custom_call_target="tpu_custom_call" | custom-call | tf_op jit(solution)/shard_map/pallas_call | solution.py:230
  26.7 8.0 %all-to-all-start = ((bf16[32,24,128]{2,1,0:T(8,128)(2,1)}), bf16[32,24,128]{2,1,0:T(8,128)(2,1)S(1)}, u32[]{:S(2)}, u32[]{:S(2)}) async-start(bf16[32,24,128]{2,1,0:T(8,128)(2,1)} %shard_map.111), calls=%async_computation | async-start | bytes 393216 | tf_op jit(solution)/shard_map/all_to_all | solution.py:235
  34.7 3.3 %collective-permute-start = (bf16[128,512]{1,0:T(8,128)(2,1)S(1)}, bf16[128,512]{1,0:T(8,128)(2,1)S(1)}, u32[]{:S(2)}, u32[]{:S(2)}) collective-permute-start(bf16[128,512]{1,0:T(8,128)(2,1)S(1)} %get-tuple-element.18), channel_id=1, source_target_pairs={{0,16},{16,32},{32,48},{48,64},{64,80},{80,96},{96,112},{112,128},... | collective-permute-start | bytes 393224 | tf_op jit(solution)/shard_map/ppermute | solution.py:186
  38.1 3.6 %all-to-all-done.recv_ref = bf16[32,24,128]{2,1,0:T(8,128)(2,1)S(1)} async-done(((bf16[32,24,128]{2,1,0:T(8,128)(2,1)}), bf16[32,24,128]{2,1,0:T(8,128)(2,1)S(1)}, u32[]{:S(2)}, u32[]{:S(2)}) %all-to-all-start) | async-done | bytes 196640 | tf_op jit(solution)/shard_map/all_to_all | solution.py:235
  41.7 0.2 shard_map.112
  41.9 16.0 %collective-permute-start.3 = (f32[16,128]{1,0:T(8,128)S(1)}, f32[16,128]{1,0:T(8,128)S(1)}, u32[]{:S(2)}, u32[]{:S(2)}) collective-permute-start(f32[16,128]{1,0:T(8,128)S(1)} %get-tuple-element.27), channel_id=1, source_target_pairs={{0,0},{1,32},{2,64},{3,96},{4,128},{5,160},{6,192},{7,224},{8,256}... | collective-permute-start | bytes 24584 | tf_op jit(solution)/shard_map/ppermute | solution.py:180
  57.9 0.0 collective-permute-done.before_ref
  58.0 4.6 %shard_map.113 = (bf16[512,512]{1,0:T(8,128)(2,1)}, bf16[512,512]{1,0:T(8,128)(2,1)}, bf16[512,512]{1,0:T(8,128)(2,1)}, bf16[512,512]{1,0:T(8,128)(2,1)}) custom-call(bf16[512,512]{1,0:T(8,128)(2,1)S(1)} %copy-done.1, bf16[512,512]{1,0:T(8,128)(2,1)S(1)} %copy-done.3, bf16[512,512]{1,0:T(8,128)(2,1)S(1)} %copy-done.5, bf16[512,512]{1,0:T(8,128)(2,1)S(1)} %copy-done.7, ...), custom_call_target="tpu_custom_call" | custom-call | tf_op jit(solution)/shard_map/pallas_call | solution.py:242
  62.6 0.0 collective-permute-done.3.refs_0_
  62.6 0.7 %shard_map.114 = (f32[8,16]{1,0:T(8,128)}, f32[1,16]{1,0:T(1,128)}) custom-call(f32[16,128]{1,0:T(8,128)S(1)} %collective-permute-done.3.refs_0_, f32[1,16]{1,0:T(1,128)S(1)} %bitcast.3), custom_call_target="tpu_custom_call" | custom-call | tf_op jit(solution)/shard_map/pallas_call | solution.py:250
  (12 shorter events, 0.0 us)
Async XLA Ops:
  0.6 0.7 %copy-start.9 = (f32[16]{0:T(128)S(1)}, f32[16]{0:T(128)}, u32[]{:S(2)}) copy-start(f32[16]{0:T(128)} %param.11) | copy-start | bytes 196
  1.3 1.0 %copy-start = (bf16[512,512]{1,0:T(8,128)(2,1)S(1)}, bf16[512,512]{1,0:T(8,128)(2,1)}, u32[]{:S(2)}) copy-start(bf16[512,512]{1,0:T(8,128)(2,1)} %key_ref.5) | copy-start | bytes 1572868
  2.3 1.0 %copy-start.2 = (bf16[512,512]{1,0:T(8,128)(2,1)S(1)}, bf16[512,512]{1,0:T(8,128)(2,1)}, u32[]{:S(2)}) copy-start(bf16[512,512]{1,0:T(8,128)(2,1)} %value_ref.5) | copy-start | bytes 1572868
  3.4 1.0 %copy-start.4 = (bf16[512,512]{1,0:T(8,128)(2,1)S(1)}, bf16[512,512]{1,0:T(8,128)(2,1)}, u32[]{:S(2)}) copy-start(bf16[512,512]{1,0:T(8,128)(2,1)} %query_ref.5) | copy-start | bytes 1572868
  4.4 1.0 %copy-start.6 = (bf16[512,512]{1,0:T(8,128)(2,1)S(1)}, bf16[512,512]{1,0:T(8,128)(2,1)}, u32[]{:S(2)}) copy-start(bf16[512,512]{1,0:T(8,128)(2,1)} %cot_ref.5) | copy-start | bytes 1572868
  5.5 0.7 %copy-start.8 = (f32[8,16]{1,0:T(8,128)S(1)}, f32[8,16]{1,0:T(8,128)}, u32[]{:S(2)}) copy-start(f32[8,16]{1,0:T(8,128)} %weight_ref.1) | copy-start | bytes 1540
  6.3 16.1 %collective-permute-start.1 = (bf16[128,512]{1,0:T(8,128)(2,1)S(1)}, bf16[128,512]{1,0:T(8,128)(2,1)S(1)}, u32[]{:S(2)}, u32[]{:S(2)}) collective-permute-start(bf16[128,512]{1,0:T(8,128)(2,1)S(1)} %get-tuple-element.19), channel_id=1, source_target_pairs={{16,0},{32,16},{48,32},{64,48},{80,64},{96,80},{112,96},{128,112},... | collective-permute-start | bytes 393224 | tf_op jit(solution)/shard_map/ppermute | solution.py:186
  8.9 17.1 %collective-permute-start.2 = (f32[8,128]{1,0:T(8,128)S(1)}, f32[8,128]{1,0:T(8,128)S(1)}, u32[]{:S(2)}, u32[]{:S(2)}) collective-permute-start(f32[8,128]{1,0:T(8,128)S(1)} %get-tuple-element.20), channel_id=1, source_target_pairs={{0,0},{1,32},{2,64},{3,96},{4,128},{5,160},{6,192},{7,224},{8,256}... | collective-permute-start | bytes 12296 | tf_op jit(solution)/shard_map/ppermute | solution.py:180
  22.5 35.5 %copy-start.3 = (bf16[512,512]{1,0:T(8,128)(2,1)S(1)}, bf16[512,512]{1,0:T(8,128)(2,1)}, u32[]{:S(2)}) copy-start(bf16[512,512]{1,0:T(8,128)(2,1)} %value_ref.5) | copy-start | bytes 1572868
  22.5 35.5 %copy-start.5 = (bf16[512,512]{1,0:T(8,128)(2,1)S(1)}, bf16[512,512]{1,0:T(8,128)(2,1)}, u32[]{:S(2)}) copy-start(bf16[512,512]{1,0:T(8,128)(2,1)} %query_ref.5) | copy-start | bytes 1572868
  22.5 35.5 %copy-start.7 = (bf16[512,512]{1,0:T(8,128)(2,1)S(1)}, bf16[512,512]{1,0:T(8,128)(2,1)}, u32[]{:S(2)}) copy-start(bf16[512,512]{1,0:T(8,128)(2,1)} %cot_ref.5) | copy-start | bytes 1572868
  26.0 32.0 %copy-start.1 = (bf16[512,512]{1,0:T(8,128)(2,1)S(1)}, bf16[512,512]{1,0:T(8,128)(2,1)}, u32[]{:S(2)}) copy-start(bf16[512,512]{1,0:T(8,128)(2,1)} %key_ref.5) | copy-start | bytes 1572868
  26.7 15.0 %all-to-all-start = ((bf16[32,24,128]{2,1,0:T(8,128)(2,1)}), bf16[32,24,128]{2,1,0:T(8,128)(2,1)S(1)}, u32[]{:S(2)}, u32[]{:S(2)}) async-start(bf16[32,24,128]{2,1,0:T(8,128)(2,1)} %shard_map.111), calls=%async_computation | async-start | bytes 393216 | tf_op jit(solution)/shard_map/all_to_all | solution.py:235
  34.7 23.2 %collective-permute-start = (bf16[128,512]{1,0:T(8,128)(2,1)S(1)}, bf16[128,512]{1,0:T(8,128)(2,1)S(1)}, u32[]{:S(2)}, u32[]{:S(2)}) collective-permute-start(bf16[128,512]{1,0:T(8,128)(2,1)S(1)} %get-tuple-element.18), channel_id=1, source_target_pairs={{0,16},{16,32},{32,48},{48,64},{64,80},{80,96},{96,112},{112,128},... | collective-permute-start | bytes 393224 | tf_op jit(solution)/shard_map/ppermute | solution.py:186
  41.9 20.7 %collective-permute-start.3 = (f32[16,128]{1,0:T(8,128)S(1)}, f32[16,128]{1,0:T(8,128)S(1)}, u32[]{:S(2)}, u32[]{:S(2)}) collective-permute-start(f32[16,128]{1,0:T(8,128)S(1)} %get-tuple-element.27), channel_id=1, source_target_pairs={{0,0},{1,32},{2,64},{3,96},{4,128},{5,160},{6,192},{7,224},{8,256}... | collective-permute-start | bytes 24584 | tf_op jit(solution)/shard_map/ppermute | solution.py:180

commit v2 on v1

--- a/solution.py
+++ b/solution.py
@@ -12,7 +12,7 @@
 LANES = 128
 F32 = jnp.float32
 BF16 = jnp.bfloat16
-VMEM_BYTES = 48 * 1024 * 1024
+MIB = 1024 * 1024
 NT = (((1,), (1,)), ((), ()))
 
 
@@ -24,44 +24,81 @@
     return (a.astype(F32) * b.astype(F32)).astype(BF16)
 
 
-def edges_kernel(key_ref, value_ref, query_ref, cot_ref, weight_ref, rate_ref, tail_ref, head_ref, taps_ref):
-    tail_ref[...] = rounded_product(key_ref[...], value_ref[...])
-    head_ref[...] = rounded_product(cot_ref[...], query_ref[...])
-    tap_count, group_count = weight_ref.shape
-    first_tap = lax.axis_index("fsdp") * tap_count
-    taps = (first_tap + iota((tap_count, group_count), 0)).astype(F32)
+def front_kernel(key, value, query, cot, weight, rate, tail_ref, head_ref, taps_ref, *scratch):
+    refs, sems = scratch[:-1], scratch[-1]
+    tail = pl.ds(key.shape[0] - FILT, FILT)
+    head = pl.ds(0, FILT)
+    sources = [weight, rate, cot.at[head], query.at[head], key.at[tail], value.at[tail]]
+    copies = [pltpu.make_async_copy(s, d, sems.at[i]) for i, (s, d) in enumerate(zip(sources, refs))]
+    for copy in copies:
+        copy.start()
+    weight_ref, rate_ref, cot_ref, query_ref, key_ref, value_ref = refs
+    copies[0].wait()
+    copies[1].wait()
+    tap_count, group_count = weight.shape
+    taps = (lax.axis_index("fsdp") * tap_count + iota((tap_count, group_count), 0)).astype(F32)
     decayed = weight_ref[...] * jnp.exp(-jnp.exp(rate_ref[...]) * taps)
     high = decayed.astype(BF16).astype(F32)
     taps_ref[...] = jnp.zeros_like(taps_ref)
     taps_ref[:, :group_count] = high
     taps_ref[:, group_count : 2 * group_count] = decayed - high
-
-
-def sums_kernel(key_ref, value_ref, query_ref, cot_ref, next_ref, sums_ref):
-    rows = key_ref.shape[0]
-    blocks = rows // FILT
-    products = rounded_product(key_ref[...], value_ref[...])
-    grads = jnp.concatenate([rounded_product(cot_ref[...], query_ref[...]), next_ref[...]], axis=0)
-    left = jnp.concatenate([products[b * FILT : (b + 1) * FILT] for b in range(blocks)], axis=1)
-    right = jnp.concatenate([grads[b * FILT : (b + 2) * FILT] for b in range(blocks)], axis=1)
+    copies[2].wait()
+    copies[3].wait()
+    head_ref[...] = rounded_product(cot_ref[...], query_ref[...])
+    copies[4].wait()
+    copies[5].wait()
+    tail_ref[...] = rounded_product(key_ref[...], value_ref[...])
+
+
+def outer_products(left, right):
     groups = LANES // GROUP
     lane_group = (iota(left.shape, 1) % LANES) // GROUP
     zero = jnp.zeros_like(left)
     stacked = jnp.concatenate([jnp.where(lane_group == g, left, zero) for g in range(groups)], axis=0)
     outer = lax.dot_general(stacked, right, NT, preferred_element_type=F32)
-    later = iota((FILT, FILT), 1) >= iota((FILT, FILT), 0)
-    rolled = jnp.zeros((groups * 8, LANES), F32)
-    merged = [
-        jnp.where(later, outer[g * FILT : (g + 1) * FILT, :FILT], outer[g * FILT : (g + 1) * FILT, FILT:])
-        for g in range(groups)
-    ]
+    return [outer[g * FILT : (g + 1) * FILT] for g in range(groups)]
+
+
+def diagonal_sums(squares):
+    rolled = jnp.zeros((len(squares) * 8, LANES), F32)
     for i in range(FILT // 8):
-        part = jnp.concatenate([m[8 * i : 8 * i + 8] for m in merged], axis=0)
+        part = jnp.concatenate([m[8 * i : 8 * i + 8] for m in squares], axis=0)
         rolled = rolled + (pltpu.roll(part, FILT - 8 * i, axis=1) if i else part)
     row = iota(rolled.shape, 0) % 8
     for step in (1, 2, 4):
         rolled = jnp.where((row & step) != 0, pltpu.roll(rolled, FILT - step, axis=1), rolled)
-    sums_ref[...] = rolled.reshape(groups, 8, LANES).sum(axis=1)
+    return rolled.reshape(len(squares), 8, LANES).sum(axis=1)
+
+
+def same_block():
+    return iota((FILT, FILT), 1) >= iota((FILT, FILT), 0)
+
+
+def sums_kernel(key_ref, value_ref, query_ref, cot_ref, sums_ref):
+    blocks = key_ref.shape[0] // FILT
+    same = same_block()
+    groups = LANES // GROUP
+    for tile in range(key_ref.shape[1] // LANES):
+        lanes = slice(tile * LANES, (tile + 1) * LANES)
+        products = rounded_product(key_ref[:, lanes], value_ref[:, lanes])
+        grads = rounded_product(cot_ref[:, lanes], query_ref[:, lanes])
+        grads = jnp.concatenate([grads, jnp.zeros((FILT, LANES), BF16)], axis=0)
+        left = jnp.concatenate([products[b * FILT : (b + 1) * FILT] for b in range(blocks)], axis=1)
+        right = jnp.concatenate([grads[b * FILT : (b + 2) * FILT] for b in range(blocks)], axis=1)
+        sums_ref[tile * groups : (tile + 1) * groups] = diagonal_sums(
+            [jnp.where(same, outer[:, :FILT], outer[:, FILT:]) for outer in outer_products(left, right)]
+        )
+
+
+def whole_sums_kernel(sums_ref, tail_ref, after_ref, out_ref):
+    same = same_block()
+    groups = LANES // GROUP
+    for tile in range(tail_ref.shape[1] // LANES):
+        lanes = slice(tile * LANES, (tile + 1) * LANES)
+        rows = slice(tile * groups, (tile + 1) * groups)
+        outers = outer_products(tail_ref[:, lanes], after_ref[:, lanes])
+        crossing = diagonal_sums([jnp.where(same, jnp.zeros_like(outer), outer) for outer in outers])
+        out_ref[rows] = sums_ref[rows] + crossing
 
 
 def message_kernel(sums_ref, taps_ref, out_ref):
@@ -74,33 +111,62 @@
         out_ref[peer] = halves[peer % 2]
 
 
+LANDING = ((0, 2, 3, 1), (0, 1, 2, 3), (0, 1, 2, 3), (2, 0, 1, 3))
+SIDE = 4
+
+
+def landing(ctx, fsdp):
+    column, half = ctx // 2, ctx % 2
+    x, hi = fsdp // SIDE, fsdp % SIDE
+    place = (x + 2) % SIDE * SIDE + LANDING[column % SIDE][hi]
+    return place * 2 + half, column
+
+
+def by_column(column, values):
+    out = values[1]
+    for q in (0, 3):
+        out = jnp.where(column % SIDE == q, values[q], out)
+    return out
+
+
+def landed_piece(ctx, column):
+    low = ctx // 2 % SIDE
+    hi = jnp.int32(0)
+    for z in range(SIDE):
+        hi = jnp.where(low == z, by_column(column, [jnp.int32(LANDING[q].index(z)) for q in range(SIDE)]), hi)
+    return (ctx // 8 + 2) % SIDE * SIDE + hi
+
+
 def reduce_kernel(recv_ref, filt_ref, flipped_ref, home_ref):
-    peers, rows, _ = recv_ref.shape
+    peers = recv_ref.shape[0]
     half = GROUP
+    own, column = lax.axis_index("ctx"), lax.axis_index("fsdp")
     total = jnp.zeros((half, LANES), F32)
-    pieces = ([], [])
+    landed = []
     for peer in range(peers):
         message = recv_ref[peer].astype(F32)
         total = total + message[:half]
-        pieces[peer % 2].append(message[half:])
-    eye = (iota((2 * half, LANES), 0) == iota((2 * half, LANES), 1)).astype(F32)
-    turned = [
-        lax.dot_general(
-            eye.astype(BF16), jnp.concatenate(p, axis=0).astype(BF16), NT, preferred_element_type=F32
-        )
-        for p in pieces
-    ]
+        landed.append(message[half:])
+    eye = (iota((2 * half, LANES), 0) == iota((2 * half, LANES), 1)).astype(BF16)
+    turned = []
+    for h in range(2):
+        pieces = []
+        for piece in range(peers // 2):
+            x, hi = piece // SIDE, piece % SIDE
+            places = [(x + 2) % SIDE * SIDE + LANDING[q][hi] for q in range(SIDE)]
+            pieces.append(by_column(column, [landed[2 * place + h] for place in places]))
+        pieces = jnp.concatenate(pieces, axis=0).astype(BF16)
+        turned.append(lax.dot_general(eye, pieces, NT, preferred_element_type=F32))
     high = jnp.concatenate([t[:half] for t in turned], axis=0)
     flip = ((iota((FILT, FILT), 0) + iota((FILT, FILT), 1)) % FILT == 0).astype(BF16)
     filt_ref[...] = high
     flipped_ref[...] = jnp.dot(high.astype(BF16), flip, preferred_element_type=F32)
-    own = lax.axis_index("ctx")
     decayed = [t[:half] + t[half:] for t in turned]
     own_decayed = jnp.where(own % 2 == 0, decayed[0], decayed[1])
     lane = iota((half, LANES), 1)
     rate = jnp.sum(own_decayed * total * lane.astype(F32), axis=1, keepdims=True)
-    tap_count = 8
-    moved = pltpu.roll(total, (FILT - tap_count * (own // 2)) % FILT, axis=1)
+    tap_count = FILT * 2 // peers
+    moved = pltpu.roll(total, (FILT - tap_count * landed_piece(own, column)) % FILT, axis=1)
     home_ref[...] = jnp.where(lane < tap_count, moved, rate)
 
 
@@ -170,14 +236,18 @@
     grad_rate_ref[...] = turned[tap_count : tap_count + 1, :group_count] * (-rates) * scale
 
 
-def params():
-    return pltpu.CompilerParams(vmem_limit_bytes=VMEM_BYTES)
-
-
-def swap_axes(value):
+def params(mib=24):
+    return pltpu.CompilerParams(vmem_limit_bytes=mib * MIB)
+
+
+def moved_pieces(value, back):
     ctx, fsdp = lax.axis_size("ctx"), lax.axis_size("fsdp")
-    pairs = [(c * fsdp + f, (2 * f + c % 2) * fsdp + c // 2) for c in range(ctx) for f in range(fsdp)]
-    return lax.ppermute(value, ("ctx", "fsdp"), pairs)
+    pairs = []
+    for c in range(ctx):
+        for f in range(fsdp):
+            there, column = landing(c, f)
+            pairs.append((c * fsdp + f, there * fsdp + column))
+    return lax.ppermute(value, ("ctx", "fsdp"), [(b, a) for a, b in pairs] if back else pairs)
 
 
 def passed_along(value, by):
@@ -196,24 +266,19 @@
     last = tokens // FILT - 1
     tap_count, tap_groups = filter_weight.shape
 
-    tail_spec = pl.BlockSpec((FILT, channels), lambda i: (last, 0))
-    head_spec = pl.BlockSpec((FILT, channels), lambda i: (0, 0))
+    anywhere = pl.BlockSpec(memory_space=pl.ANY)
+    edge = (FILT, channels)
     tail, head, taps = pl.pallas_call(
-        edges_kernel,
-        grid=(1,),
-        in_specs=[
-            tail_spec, tail_spec, head_spec, head_spec,
-            pl.BlockSpec(filter_weight.shape, lambda i: (0, 0)),
-            pl.BlockSpec(rate_row.shape, lambda i: (0, 0)),
-        ],
-        out_specs=[head_spec, head_spec, pl.BlockSpec((tap_count, LANES), lambda i: (0, 0))],
-        out_shape=[
-            sds((FILT, channels), BF16), sds((FILT, channels), BF16), sds((tap_count, LANES), F32),
-        ],
-        compiler_params=params(),
+        front_kernel,
+        in_specs=[anywhere] * 6,
+        out_shape=[sds(edge, BF16), sds(edge, BF16), sds((tap_count, LANES), F32)],
+        scratch_shapes=[pltpu.VMEM(filter_weight.shape, F32), pltpu.VMEM(rate_row.shape, F32)]
+        + [pltpu.VMEM(edge, BF16)] * 4
+        + [pltpu.SemaphoreType.DMA((6,))],
+        compiler_params=params(60),
     )(key_in, value_in, query, cotangent, filter_weight, rate_row)
     after = passed_along(head, -1)
-    taps_here = swap_axes(taps)
+    taps_here = moved_pieces(taps, False)
     before = passed_along(tail, 1)
 
     tile = pl.BlockSpec((tokens, LANES), lambda i: (0, i))
@@ -221,12 +286,14 @@
     group_rows = pl.BlockSpec((LANES // GROUP, LANES), lambda i: (i, 0))
     sums = pl.pallas_call(
         sums_kernel,
-        grid=(channels // LANES,),
-        in_specs=[tile, tile, tile, tile, halo],
-        out_specs=group_rows,
         out_shape=sds((groups, LANES), F32),
         compiler_params=params(),
-    )(key_in, value_in, query, cotangent, after)
+    )(key_in, value_in, query, cotangent)
+    sums = pl.pallas_call(
+        whole_sums_kernel,
+        out_shape=sds((groups, LANES), F32),
+        compiler_params=params(),
+    )(sums, tail, after)
     message = pl.pallas_call(
         message_kernel,
         out_shape=sds((peers, groups // 2 + tap_count, LANES), BF16),
@@ -238,7 +305,7 @@
         out_shape=[sds((groups, LANES), F32), sds((groups, LANES), F32), sds((groups // 2, LANES), F32)],
         compiler_params=params(),
     )(received)
-    home = swap_axes(home)
+    home = moved_pieces(home, True)
     output, grad_query, grad_key, grad_value = pl.pallas_call(
         outputs_kernel,
         grid=(channels // LANES,),

time: 63.7 us -> 58.3 us (0.915)
  the two profiles are of different devices: /device:TPU:73 before, /device:TPU:105 now
where the time goes in v2:
time: 58.3 us; the launch traced here: 58 us
  starting transfers between devices  42.5 us (73%)
  Pallas kernels  10.9 us (19%)
  waiting for transfers between devices  3.74 us (6%)
  between operations  0.81 us (1%)
    ppermute x2, starting transfers between devices, moved_pieces(): lax.ppermute(value, ('ctx', 'fsdp'), [(b, a) for a, b in pairs] if back e...  25.9 us
    all_to_all x1, starting transfers between devices, per_device(): received = lax.all_to_all(message, 'ctx', 0, 0, tiled=True)  10.7 us
    ppermute x2, starting transfers between devices, passed_along(): return lax.ppermute(value, 'ctx', pairs)  5.92 us
    pallas_call x1, Pallas kernels, per_device(): pl.pallas_call(outputs_kernel, grid=(channels // LANES,), in_specs=[tile,...  4.59 us
    all_to_all x1, waiting for transfers between devices, per_device(): received = lax.all_to_all(message, 'ctx', 0, 0, tiled=True)  3.73 us
    pallas_call x1, Pallas kernels, per_device(): pl.pallas_call(front_kernel, in_specs=[anywhere] * 6, out_shape=[sds(edge...  2.02 us
    pallas_call x1, Pallas kernels, per_device(): pl.pallas_call(sums_kernel, out_shape=sds((groups, LANES), F32), compiler...  1.61 us
  transfers between devices with their start and end apart: 5, of which 1 were waited for; matrix products, arithmetic and copies ran while one was open for 0% of the time, Pallas kernels for 13%

profile of v2, /device:TPU:105, one launch (start us, length us, event | category | flops | bytes accessed | tf_op | source)
XLA Modules:
  0.0 58.0 jit_solution(3337068315183561984)
XLA Ops:
  0.6 0.0 copy-start
  0.6 0.0 copy-start.1
  0.7 0.0 copy-start.2
  0.7 0.0 copy-start.3
  0.7 2.0 %shard_map.109 = (bf16[128,512]{1,0:T(8,128)(2,1)}, bf16[128,512]{1,0:T(8,128)(2,1)}, f32[8,128]{1,0:T(8,128)}) custom-call(bf16[512,512]{1,0:T(8,128)(2,1)} %key_ref.3, bf16[512,512]{1,0:T(8,128)(2,1)} %value_ref.3, bf16[512,512]{1,0:T(8,128)(2,1)} %query_ref.3, bf16[512,512]{1,0:T(8,128)(2,1)} %cot_ref.3, f32[8,16]{1,0:T(8,128)} %weight.1, f32[1,16]{1,0:T(1,128)} %bitcast.2), custom_call_target="tpu_custom_call" | custom-call | tf_op jit(solution)/shard_map/pallas_call | solution.py:271
  2.7 2.6 %collective-permute-start.1 = (bf16[128,512]{1,0:T(8,128)(2,1)}, bf16[128,512]{1,0:T(8,128)(2,1)S(1)}, u32[]{:S(2)}, u32[]{:S(2)}) collective-permute-start(bf16[128,512]{1,0:T(8,128)(2,1)} %get-tuple-element.19), channel_id=1, source_target_pairs={{16,0},{32,16},{48,32},{64,48},{80,64},{96,80},{112,96},{128,112},... | collective-permute-start | bytes 393224 | tf_op jit(solution)/shard_map/ppermute | solution.py:256
  5.3 0.0 copy-start.4
  5.3 12.3 %collective-permute-start.2 = (f32[8,128]{1,0:T(8,128)}, f32[8,128]{1,0:T(8,128)S(1)}, u32[]{:S(2)}, u32[]{:S(2)}) collective-permute-start(f32[8,128]{1,0:T(8,128)} %get-tuple-element.20), channel_id=1, source_target_pairs={{0,256},{1,320},{2,352},{3,288},{4,384},{5,448},{6,480},{7,416},{8... | collective-permute-start | bytes 12296 | tf_op jit(solution)/shard_map/ppermute | solution.py:250
  17.6 0.0 copy-done
  17.6 1.6 %shard_map.110.sums_ref = f32[32,128]{1,0:T(8,128)S(1)} custom-call(bf16[512,512]{1,0:T(8,128)(2,1)S(1)} %copy-done, bf16[512,512]{1,0:T(8,128)(2,1)S(1)} %copy-done.1, bf16[512,512]{1,0:T(8,128)(2,1)S(1)} %copy-done.2, bf16[512,512]{1,0:T(8,128)(2,1)S(1)} %copy-done.3), custom_call_target="tpu_custom_call" | custom-call | tf_op jit(solution)/shard_map/pallas_call | solution.py:287
  19.2 0.0 collective-permute-done.1.after_ref
  19.3 1.1 %shard_map.111.sums_ref = f32[32,128]{1,0:T(8,128)S(1)} custom-call(f32[32,128]{1,0:T(8,128)S(1)} %shard_map.110.sums_ref, bf16[128,512]{1,0:T(8,128)(2,1)S(1)} %copy-done.4, bf16[128,512]{1,0:T(8,128)(2,1)S(1)} %collective-permute-done.1.after_ref), custom_call_target="tpu_custom_call" | custom-call | tf_op jit(solution)/shard_map/pallas_call | solution.py:292
  20.4 0.0 collective-permute-done.2.taps_ref
  20.4 0.7 %shard_map.112 = bf16[32,24,128]{2,1,0:T(8,128)(2,1)} custom-call(f32[32,128]{1,0:T(8,128)S(1)} %shard_map.111.sums_ref, f32[8,128]{1,0:T(8,128)S(1)} %collective-permute-done.2.taps_ref), custom_call_target="tpu_custom_call" | custom-call | tf_op jit(solution)/shard_map/pallas_call | solution.py:297
  21.1 10.7 %all-to-all-start = ((bf16[32,24,128]{2,1,0:T(8,128)(2,1)}), bf16[32,24,128]{2,1,0:T(8,128)(2,1)S(1)}, u32[]{:S(2)}, u32[]{:S(2)}) async-start(bf16[32,24,128]{2,1,0:T(8,128)(2,1)} %shard_map.112), calls=%async_computation | async-start | bytes 393216 | tf_op jit(solution)/shard_map/all_to_all | solution.py:302
  31.8 3.3 %collective-permute-start = (bf16[128,512]{1,0:T(8,128)(2,1)S(1)}, bf16[128,512]{1,0:T(8,128)(2,1)S(1)}, u32[]{:S(2)}, u32[]{:S(2)}) collective-permute-start(bf16[128,512]{1,0:T(8,128)(2,1)S(1)} %copy-done.4), channel_id=1, source_target_pairs={{0,16},{16,32},{32,48},{48,64},{64,80},{80,96},{96,112},{112,128},... | collective-permute-start | bytes 393224 | tf_op jit(solution)/shard_map/ppermute | solution.py:256
  35.1 3.7 %all-to-all-done.recv_ref = bf16[32,24,128]{2,1,0:T(8,128)(2,1)S(1)} async-done(((bf16[32,24,128]{2,1,0:T(8,128)(2,1)}), bf16[32,24,128]{2,1,0:T(8,128)(2,1)S(1)}, u32[]{:S(2)}, u32[]{:S(2)}) %all-to-all-start) | async-done | bytes 196640 | tf_op jit(solution)/shard_map/all_to_all | solution.py:302
  38.9 0.2 shard_map.113
  39.1 13.6 %collective-permute-start.3 = (f32[16,128]{1,0:T(8,128)S(1)}, f32[16,128]{1,0:T(8,128)S(1)}, u32[]{:S(2)}, u32[]{:S(2)}) collective-permute-start(f32[16,128]{1,0:T(8,128)S(1)} %get-tuple-element.27), channel_id=1, source_target_pairs={{256,0},{320,1},{352,2},{288,3},{384,4},{448,5},{480,6},{416,7},{0... | collective-permute-start | bytes 24584 | tf_op jit(solution)/shard_map/ppermute | solution.py:250
  52.7 0.0 collective-permute-done.before_ref
  52.7 0.0 copy-start.5
  52.7 4.6 %shard_map.114 = (bf16[512,512]{1,0:T(8,128)(2,1)}, bf16[512,512]{1,0:T(8,128)(2,1)}, bf16[512,512]{1,0:T(8,128)(2,1)}, bf16[512,512]{1,0:T(8,128)(2,1)}) custom-call(bf16[512,512]{1,0:T(8,128)(2,1)S(1)} %copy-done, bf16[512,512]{1,0:T(8,128)(2,1)S(1)} %copy-done.1, bf16[512,512]{1,0:T(8,128)(2,1)S(1)} %copy-done.2, bf16[512,512]{1,0:T(8,128)(2,1)S(1)} %copy-done.3, ...), custom_call_target="tpu_custom_call" | custom-call | tf_op jit(solution)/shard_map/pallas_call | solution.py:309
  57.3 0.0 collective-permute-done.3.refs_0_
  57.3 0.7 %shard_map.115 = (f32[8,16]{1,0:T(8,128)}, f32[1,16]{1,0:T(1,128)}) custom-call(f32[16,128]{1,0:T(8,128)S(1)} %collective-permute-done.3.refs_0_, f32[1,16]{1,0:T(1,128)S(1)} %bitcast.3), custom_call_target="tpu_custom_call" | custom-call | tf_op jit(solution)/shard_map/pallas_call | solution.py:317
  (5 shorter events, 0.0 us)
Async XLA Ops:
  0.6 17.0 %copy-start = (bf16[512,512]{1,0:T(8,128)(2,1)S(1)}, bf16[512,512]{1,0:T(8,128)(2,1)}, u32[]{:S(2)}) copy-start(bf16[512,512]{1,0:T(8,128)(2,1)} %key_ref.3) | copy-start | bytes 1572868
  0.6 17.0 %copy-start.1 = (bf16[512,512]{1,0:T(8,128)(2,1)S(1)}, bf16[512,512]{1,0:T(8,128)(2,1)}, u32[]{:S(2)}) copy-start(bf16[512,512]{1,0:T(8,128)(2,1)} %value_ref.3) | copy-start | bytes 1572868
  0.7 17.0 %copy-start.2 = (bf16[512,512]{1,0:T(8,128)(2,1)S(1)}, bf16[512,512]{1,0:T(8,128)(2,1)}, u32[]{:S(2)}) copy-start(bf16[512,512]{1,0:T(8,128)(2,1)} %query_ref.3) | copy-start | bytes 1572868
  0.7 17.0 %copy-start.3 = (bf16[512,512]{1,0:T(8,128)(2,1)S(1)}, bf16[512,512]{1,0:T(8,128)(2,1)}, u32[]{:S(2)}) copy-start(bf16[512,512]{1,0:T(8,128)(2,1)} %cot_ref.3) | copy-start | bytes 1572868
  2.7 16.5 %collective-permute-start.1 = (bf16[128,512]{1,0:T(8,128)(2,1)}, bf16[128,512]{1,0:T(8,128)(2,1)S(1)}, u32[]{:S(2)}, u32[]{:S(2)}) collective-permute-start(bf16[128,512]{1,0:T(8,128)(2,1)} %get-tuple-element.19), channel_id=1, source_target_pairs={{16,0},{32,16},{48,32},{64,48},{80,64},{96,80},{112,96},{128,112},... | collective-permute-start | bytes 393224 | tf_op jit(solution)/shard_map/ppermute | solution.py:256
  5.3 14.0 %copy-start.4 = (bf16[128,512]{1,0:T(8,128)(2,1)S(1)}, bf16[128,512]{1,0:T(8,128)(2,1)}, u32[]{:S(2)}) copy-start(bf16[128,512]{1,0:T(8,128)(2,1)} %get-tuple-element.18.tail_ref) | copy-start | bytes 393220
  5.3 15.1 %collective-permute-start.2 = (f32[8,128]{1,0:T(8,128)}, f32[8,128]{1,0:T(8,128)S(1)}, u32[]{:S(2)}, u32[]{:S(2)}) collective-permute-start(f32[8,128]{1,0:T(8,128)} %get-tuple-element.20), channel_id=1, source_target_pairs={{0,256},{1,320},{2,352},{3,288},{4,384},{5,448},{6,480},{7,416},{8... | collective-permute-start | bytes 12296 | tf_op jit(solution)/shard_map/ppermute | solution.py:250
  21.1 17.7 %all-to-all-start = ((bf16[32,24,128]{2,1,0:T(8,128)(2,1)}), bf16[32,24,128]{2,1,0:T(8,128)(2,1)S(1)}, u32[]{:S(2)}, u32[]{:S(2)}) async-start(bf16[32,24,128]{2,1,0:T(8,128)(2,1)} %shard_map.112), calls=%async_computation | async-start | bytes 393216 | tf_op jit(solution)/shard_map/all_to_all | solution.py:302
  31.8 20.9 %collective-permute-start = (bf16[128,512]{1,0:T(8,128)(2,1)S(1)}, bf16[128,512]{1,0:T(8,128)(2,1)S(1)}, u32[]{:S(2)}, u32[]{:S(2)}) collective-permute-start(bf16[128,512]{1,0:T(8,128)(2,1)S(1)} %copy-done.4), channel_id=1, source_target_pairs={{0,16},{16,32},{32,48},{48,64},{64,80},{80,96},{96,112},{112,128},... | collective-permute-start | bytes 393224 | tf_op jit(solution)/shard_map/ppermute | solution.py:256
  39.1 18.2 %collective-permute-start.3 = (f32[16,128]{1,0:T(8,128)S(1)}, f32[16,128]{1,0:T(8,128)S(1)}, u32[]{:S(2)}, u32[]{:S(2)}) collective-permute-start(f32[16,128]{1,0:T(8,128)S(1)} %get-tuple-element.27), channel_id=1, source_target_pairs={{256,0},{320,1},{352,2},{288,3},{384,4},{448,5},{480,6},{416,7},{0... | collective-permute-start | bytes 24584 | tf_op jit(solution)/shard_map/ppermute | solution.py:250
  52.7 4.6 %copy-start.5 = (f32[16]{0:T(128)S(1)}, f32[16]{0:T(128)}, u32[]{:S(2)}) copy-start(f32[16]{0:T(128)} %param.11) | copy-start | bytes 196

commit v3 on v2

--- a/solution.py
+++ b/solution.py
@@ -24,30 +24,36 @@
     return (a.astype(F32) * b.astype(F32)).astype(BF16)
 
 
-def front_kernel(key, value, query, cot, weight, rate, tail_ref, head_ref, taps_ref, *scratch):
+def is_even():
+    return lax.axis_index("ctx") % 2 == 0
+
+
+def edge_rows(key, value, query, cot):
+    tail, head = rounded_product(key, value), rounded_product(cot, query)
+    return jnp.where(is_even(), tail, head), jnp.where(is_even(), head, tail)
+
+
+def front_kernel(key, value, query, cot, weight, rate, near_ref, far_ref, taps_ref, *scratch):
     refs, sems = scratch[:-1], scratch[-1]
     tail = pl.ds(key.shape[0] - FILT, FILT)
     head = pl.ds(0, FILT)
-    sources = [weight, rate, cot.at[head], query.at[head], key.at[tail], value.at[tail]]
+    sources = [weight, rate, key.at[tail], value.at[tail], query.at[head], cot.at[head]]
     copies = [pltpu.make_async_copy(s, d, sems.at[i]) for i, (s, d) in enumerate(zip(sources, refs))]
     for copy in copies:
         copy.start()
-    weight_ref, rate_ref, cot_ref, query_ref, key_ref, value_ref = refs
-    copies[0].wait()
-    copies[1].wait()
+    weight_ref, rate_ref = refs[:2]
     tap_count, group_count = weight.shape
     taps = (lax.axis_index("fsdp") * tap_count + iota((tap_count, group_count), 0)).astype(F32)
+    taps_ref[...] = jnp.zeros_like(taps_ref)
+    for copy in copies[:2]:
+        copy.wait()
     decayed = weight_ref[...] * jnp.exp(-jnp.exp(rate_ref[...]) * taps)
     high = decayed.astype(BF16).astype(F32)
-    taps_ref[...] = jnp.zeros_like(taps_ref)
     taps_ref[:, :group_count] = high
     taps_ref[:, group_count : 2 * group_count] = decayed - high
-    copies[2].wait()
-    copies[3].wait()
-    head_ref[...] = rounded_product(cot_ref[...], query_ref[...])
-    copies[4].wait()
-    copies[5].wait()
-    tail_ref[...] = rounded_product(key_ref[...], value_ref[...])
+    for copy in copies[2:]:
+        copy.wait()
+    near_ref[...], far_ref[...] = edge_rows(*(ref[...] for ref in refs[2:]))
 
 
 def outer_products(left, right):
@@ -90,13 +96,15 @@
         )
 
 
-def whole_sums_kernel(sums_ref, tail_ref, after_ref, out_ref):
+def whole_sums_kernel(sums_ref, own_near_ref, own_far_ref, far_ref, near_ref, out_ref):
     same = same_block()
     groups = LANES // GROUP
-    for tile in range(tail_ref.shape[1] // LANES):
+    for tile in range(own_near_ref.shape[1] // LANES):
         lanes = slice(tile * LANES, (tile + 1) * LANES)
         rows = slice(tile * groups, (tile + 1) * groups)
-        outers = outer_products(tail_ref[:, lanes], after_ref[:, lanes])
+        tail = jnp.where(is_even(), own_near_ref[:, lanes], own_far_ref[:, lanes])
+        after = jnp.where(is_even(), near_ref[:, lanes], far_ref[:, lanes])
+        outers = outer_products(tail, after)
         crossing = diagonal_sums([jnp.where(same, jnp.zeros_like(outer), outer) for outer in outers])
         out_ref[rows] = sums_ref[rows] + crossing
 
@@ -202,7 +210,7 @@
 
 
 def outputs_kernel(
-    key_ref, value_ref, query_ref, cot_ref, before_ref, after_ref, filt_ref, flipped_ref,
+    key_ref, value_ref, query_ref, cot_ref, far_ref, near_ref, filt_ref, flipped_ref,
     output_ref, grad_query_ref, grad_key_ref, grad_value_ref,
 ):
     blocks = key_ref.shape[0] // FILT
@@ -212,13 +220,15 @@
     above, lower = row < col, row >= col
     key, value = key_ref[...].astype(F32), value_ref[...].astype(F32)
     query, cot = query_ref[...].astype(F32), cot_ref[...].astype(F32)
-    products = jnp.concatenate([before_ref[...], (key * value).astype(BF16)], axis=0)
+    before = jnp.where(is_even(), far_ref[...], near_ref[...])
+    after = jnp.where(is_even(), near_ref[...], far_ref[...])
+    products = jnp.concatenate([before, (key * value).astype(BF16)], axis=0)
     forward = banded_pair(flipped_ref[...], above, lower)
     for b, mixed in enumerate(apply_filters(forward, products, blocks)):
         rows = slice(b * FILT, (b + 1) * FILT)
         output_ref[rows] = (query[rows] * mixed).astype(BF16)
         grad_query_ref[rows] = (cot[rows] * mixed).astype(BF16)
-    grads = jnp.concatenate([(cot * query).astype(BF16), after_ref[...]], axis=0)
+    grads = jnp.concatenate([(cot * query).astype(BF16), after], axis=0)
     backward = banded_pair(filt_ref[...], row <= col, row > col)
     for b, back in enumerate(apply_filters(backward, grads, blocks)):
         rows = slice(b * FILT, (b + 1) * FILT)
@@ -236,8 +246,16 @@
     grad_rate_ref[...] = turned[tap_count : tap_count + 1, :group_count] * (-rates) * scale
 
 
+def in_hbm(value):
+    return pltpu.with_memory_space_constraint(value, pltpu.HBM)
+
+
 def params(mib=24):
     return pltpu.CompilerParams(vmem_limit_bytes=mib * MIB)
+
+
+def cost(us):
+    return pl.CostEstimate(flops=int(us * 1e9), bytes_accessed=int(us * 3_000_000), transcendentals=0)
 
 
 def moved_pieces(value, back):
@@ -250,9 +268,11 @@
     return lax.ppermute(value, ("ctx", "fsdp"), [(b, a) for a, b in pairs] if back else pairs)
 
 
-def passed_along(value, by):
+def swapped(value, first):
     peers = lax.axis_size("ctx")
-    pairs = [(i, i + by) for i in range(peers) if 0 <= i + by < peers]
+    pairs = []
+    for i in range(first, peers - 1, 2):
+        pairs += [(i, i + 1), (i + 1, i)]
     return lax.ppermute(value, "ctx", pairs)
 
 
@@ -263,23 +283,20 @@
     scale = 1.0 / math.sqrt(tokens * peers * GROUP)
     rate_row = log_rate.reshape(1, -1)
     sds = jax.ShapeDtypeStruct
-    last = tokens // FILT - 1
     tap_count, tap_groups = filter_weight.shape
 
-    anywhere = pl.BlockSpec(memory_space=pl.ANY)
     edge = (FILT, channels)
-    tail, head, taps = pl.pallas_call(
+    own_near, own_far, taps = pl.pallas_call(
         front_kernel,
-        in_specs=[anywhere] * 6,
+        in_specs=[pl.BlockSpec(memory_space=pl.ANY)] * 6,
         out_shape=[sds(edge, BF16), sds(edge, BF16), sds((tap_count, LANES), F32)],
         scratch_shapes=[pltpu.VMEM(filter_weight.shape, F32), pltpu.VMEM(rate_row.shape, F32)]
         + [pltpu.VMEM(edge, BF16)] * 4
         + [pltpu.SemaphoreType.DMA((6,))],
-        compiler_params=params(60),
-    )(key_in, value_in, query, cotangent, filter_weight, rate_row)
-    after = passed_along(head, -1)
+        compiler_params=params(),
+    )(*(in_hbm(x) for x in (key_in, value_in, query, cotangent, filter_weight, rate_row)))
     taps_here = moved_pieces(taps, False)
-    before = passed_along(tail, 1)
+    far = swapped(own_far, 1)
 
     tile = pl.BlockSpec((tokens, LANES), lambda i: (0, i))
     halo = pl.BlockSpec((FILT, LANES), lambda i: (0, i))
@@ -287,16 +304,17 @@
     sums = pl.pallas_call(
         sums_kernel,
         out_shape=sds((groups, LANES), F32),
-        compiler_params=params(),
+        cost_estimate=cost(3), compiler_params=params(),
     )(key_in, value_in, query, cotangent)
+    near = swapped(own_near, 0)
     sums = pl.pallas_call(
         whole_sums_kernel,
         out_shape=sds((groups, LANES), F32),
         compiler_params=params(),
-    )(sums, tail, after)
+    )(sums, own_near, own_far, far, near)
     message = pl.pallas_call(
         message_kernel,
-        out_shape=sds((peers, groups // 2 + tap_count, LANES), BF16),
+        out_shape=pltpu.VMEM((peers, groups // 2 + tap_count, LANES), BF16),
         compiler_params=params(),
     )(sums, taps_here)
     received = lax.all_to_all(message, "ctx", 0, 0, tiled=True)
@@ -313,7 +331,7 @@
         out_specs=[tile] * 4,
         out_shape=[sds((tokens, channels), BF16)] * 4,
         compiler_params=params(),
-    )(key_in, value_in, query, cotangent, before, after, filt, flipped)
+    )(key_in, value_in, query, cotangent, far, near, filt, flipped)
     grad_filter, grad_rate = pl.pallas_call(
         lambda *refs: finish_kernel(*refs, scale=scale),
         out_shape=[sds(filter_weight.shape, F32), sds(rate_row.shape, F32)],

time: 58.3 us -> 56.6 us (0.971)
  the two profiles are of different devices: /device:TPU:105 before, /device:TPU:64 now
where the time goes in v3:
time: 56.6 us; the launch traced here: 56.3 us
  starting transfers between devices  24.5 us (43%)
  blocking collectives  15.4 us (27%)
  Pallas kernels  9.65 us (17%)
  waiting for transfers between devices  6.05 us (11%)
  between operations  0.78 us (1%)
    ppermute x2, starting transfers between devices, moved_pieces(): lax.ppermute(value, ('ctx', 'fsdp'), [(b, a) for a, b in pairs] if back e...  20.6 us
    all_to_all x1, blocking collectives, per_device(): received = lax.all_to_all(message, 'ctx', 0, 0, tiled=True)  15.4 us
    ppermute x2, waiting for transfers between devices, moved_pieces(): lax.ppermute(value, ('ctx', 'fsdp'), [(b, a) for a, b in pairs] if back e...  5.28 us
    pallas_call x1, Pallas kernels, per_device(): pl.pallas_call(outputs_kernel, grid=(channels // LANES,), in_specs=[tile,...  4.66 us
    ppermute x2, starting transfers between devices, swapped(): return lax.ppermute(value, 'ctx', pairs)  3.84 us
    pallas_call x1, Pallas kernels, per_device(): pl.pallas_call(sums_kernel, out_shape=sds((groups, LANES), F32), cost_est...  1.61 us
    pallas_call x1, Pallas kernels, per_device(): pl.pallas_call(front_kernel, in_specs=[pl.BlockSpec(memory_space=pl.ANY)]...  1.4 us
  transfers between devices with their start and end apart: 4, of which 2 were waited for; matrix products, arithmetic and copies ran while one was open for 0% of the time, Pallas kernels for 13%

profile of v3, /device:TPU:64, one launch (start us, length us, event | category | flops | bytes accessed | tf_op | source)
XLA Modules:
  0.0 56.3 jit_solution(6178888713671810752)
XLA Ops:
  0.6 0.0 copy-start
  0.6 0.0 copy-start.1
  0.7 0.0 copy-start.2
  0.7 0.0 copy-start.3
  0.7 1.4 %shard_map.109 = (bf16[128,512]{1,0:T(8,128)(2,1)S(1)}, bf16[128,512]{1,0:T(8,128)(2,1)S(1)}, f32[8,128]{1,0:T(8,128)S(1)}) custom-call(bf16[512,512]{1,0:T(8,128)(2,1)} %key_ref.3, bf16[512,512]{1,0:T(8,128)(2,1)} %value_ref.3, bf16[512,512]{1,0:T(8,128)(2,1)} %query_ref.3, bf16[512,512]{1,0:T(8,128)(2,1)} %cot_ref.3, f32[8,16]{1,0:T(8,128)} %weight.1, ...), custom_call_target="tpu_custom_call" | custom-call | tf_op jit(solution)/shard_map/pallas_call | solution.py:289
  2.1 15.6 %collective-permute-start.2 = (f32[8,128]{1,0:T(8,128)S(1)}, f32[8,128]{1,0:T(8,128)S(1)}, u32[]{:S(2)}, u32[]{:S(2)}) collective-permute-start(f32[8,128]{1,0:T(8,128)S(1)} %get-tuple-element.20), channel_id=1, source_target_pairs={{0,256},{1,320},{2,352},{3,288},{4,384},{5,448},{6,480},{7,416},{8... | collective-permute-start | bytes 12296 | tf_op jit(solution)/shard_map/ppermute | solution.py:268
  17.7 1.9 %collective-permute-start = (bf16[128,512]{1,0:T(8,128)(2,1)S(1)}, bf16[128,512]{1,0:T(8,128)(2,1)S(1)}, u32[]{:S(2)}, u32[]{:S(2)}) collective-permute-start(bf16[128,512]{1,0:T(8,128)(2,1)S(1)} %get-tuple-element.18.own_far_ref), channel_id=1, source_target_pairs={{16,32},{32,16},{48,64},{64,48},{80,96},{96,80},{112,128},{128,112... | collective-permute-start | bytes 393224 | tf_op jit(solution)/shard_map/ppermute | solution.py:276
  19.7 1.9 %collective-permute-start.1 = (bf16[128,512]{1,0:T(8,128)(2,1)S(1)}, bf16[128,512]{1,0:T(8,128)(2,1)S(1)}, u32[]{:S(2)}, u32[]{:S(2)}) collective-permute-start(bf16[128,512]{1,0:T(8,128)(2,1)S(1)} %get-tuple-element.19.own_near_ref), channel_id=1, source_target_pairs={{0,16},{16,0},{32,48},{48,32},{64,80},{80,64},{96,112},{112,96},{1... | collective-permute-start | bytes 393224 | tf_op jit(solution)/shard_map/ppermute | solution.py:276
  21.6 0.0 copy-done
  21.6 0.0 copy-done.1
  21.6 0.0 copy-done.2
  21.6 0.0 copy-done.3
  21.6 1.6 %shard_map.110.sums_ref = f32[32,128]{1,0:T(8,128)S(1)} custom-call(bf16[512,512]{1,0:T(8,128)(2,1)S(1)} %copy-done, bf16[512,512]{1,0:T(8,128)(2,1)S(1)} %copy-done.1, bf16[512,512]{1,0:T(8,128)(2,1)S(1)} %copy-done.2, bf16[512,512]{1,0:T(8,128)(2,1)S(1)} %copy-done.3), custom_call_target="tpu_custom_call" | custom-call | flops 3000000000 | bytes 9000000 | tf_op jit(solution)/shard_map/pallas_call | solution.py:304
  23.2 0.8 %collective-permute-done.far_ref = bf16[128,512]{1,0:T(8,128)(2,1)S(1)} collective-permute-done((bf16[128,512]{1,0:T(8,128)(2,1)S(1)}, bf16[128,512]{1,0:T(8,128)(2,1)S(1)}, u32[]{:S(2)}, u32[]{:S(2)}) %collective-permute-start) | collective-permute-done | bytes 131104 | tf_op jit(solution)/shard_map/ppermute | solution.py:276
  24.0 0.0 collective-permute-done.1.near_ref
  24.0 1.1 %shard_map.111.sums_ref = f32[32,128]{1,0:T(8,128)S(1)} custom-call(f32[32,128]{1,0:T(8,128)S(1)} %shard_map.110.sums_ref, bf16[128,512]{1,0:T(8,128)(2,1)S(1)} %get-tuple-element.19.own_near_ref, bf16[128,512]{1,0:T(8,128)(2,1)S(1)} %get-tuple-element.18.own_far_ref, bf16[128,512]{1,0:T(8,128)(2,1)S(1)} %collective-permute-done.far_ref, ...), custom_call_target="tpu_custom_call" | custom-call | tf_op jit(solution)/shard_map/pallas_call | solution.py:310
  25.1 0.0 collective-permute-done.2.taps_ref
  25.2 15.4 %all_to_all.5.recv_ref = bf16[32,24,128]{2,1,0:T(8,128)(2,1)S(1)} all-to-all(bf16[32,24,128]{2,1,0:T(8,128)(2,1)S(1)} %shard_map.112), channel_id=1, replica_groups=mesh['ctx'=32,'fsdp'=16] {'ctx'}, dimensions={0} | all-to-all | bytes 393216 | tf_op jit(solution)/shard_map/all_to_all | solution.py:320
  40.5 0.2 shard_map.113
  40.7 5.0 %collective-permute-start.3 = (f32[16,128]{1,0:T(8,128)S(1)}, f32[16,128]{1,0:T(8,128)S(1)}, u32[]{:S(2)}, u32[]{:S(2)}) collective-permute-start(f32[16,128]{1,0:T(8,128)S(1)} %get-tuple-element.27), channel_id=1, source_target_pairs={{256,0},{320,1},{352,2},{288,3},{384,4},{448,5},{480,6},{416,7},{0... | collective-permute-start | bytes 24584 | tf_op jit(solution)/shard_map/ppermute | solution.py:268
  45.7 0.0 copy-start.4
  45.7 4.7 %shard_map.114 = (bf16[512,512]{1,0:T(8,128)(2,1)}, bf16[512,512]{1,0:T(8,128)(2,1)}, bf16[512,512]{1,0:T(8,128)(2,1)}, bf16[512,512]{1,0:T(8,128)(2,1)}) custom-call(bf16[512,512]{1,0:T(8,128)(2,1)S(1)} %copy-done, bf16[512,512]{1,0:T(8,128)(2,1)S(1)} %copy-done.1, bf16[512,512]{1,0:T(8,128)(2,1)S(1)} %copy-done.2, bf16[512,512]{1,0:T(8,128)(2,1)S(1)} %copy-done.3, ...), custom_call_target="tpu_custom_call" | custom-call | tf_op jit(solution)/shard_map/pallas_call | solution.py:327
  50.4 5.3 %collective-permute-done.3.refs_0_ = f32[16,128]{1,0:T(8,128)S(1)} collective-permute-done((f32[16,128]{1,0:T(8,128)S(1)}, f32[16,128]{1,0:T(8,128)S(1)}, u32[]{:S(2)}, u32[]{:S(2)}) %collective-permute-start.3) | collective-permute-done | bytes 8224 | tf_op jit(solution)/shard_map/ppermute | solution.py:268
  55.6 0.7 %shard_map.115 = (f32[8,16]{1,0:T(8,128)}, f32[1,16]{1,0:T(1,128)}) custom-call(f32[16,128]{1,0:T(8,128)S(1)} %collective-permute-done.3.refs_0_, f32[1,16]{1,0:T(1,128)S(1)} %bitcast.3), custom_call_target="tpu_custom_call" | custom-call | tf_op jit(solution)/shard_map/pallas_call | solution.py:335
  (2 shorter events, 0.0 us)
Async XLA Ops:
  0.6 21.0 %copy-start = (bf16[512,512]{1,0:T(8,128)(2,1)S(1)}, bf16[512,512]{1,0:T(8,128)(2,1)}, u32[]{:S(2)}) copy-start(bf16[512,512]{1,0:T(8,128)(2,1)} %key_ref.3) | copy-start | bytes 1572868
  0.6 21.0 %copy-start.1 = (bf16[512,512]{1,0:T(8,128)(2,1)S(1)}, bf16[512,512]{1,0:T(8,128)(2,1)}, u32[]{:S(2)}) copy-start(bf16[512,512]{1,0:T(8,128)(2,1)} %value_ref.3) | copy-start | bytes 1572868
  0.7 21.0 %copy-start.2 = (bf16[512,512]{1,0:T(8,128)(2,1)S(1)}, bf16[512,512]{1,0:T(8,128)(2,1)}, u32[]{:S(2)}) copy-start(bf16[512,512]{1,0:T(8,128)(2,1)} %query_ref.3) | copy-start | bytes 1572868
  0.7 21.0 %copy-start.3 = (bf16[512,512]{1,0:T(8,128)(2,1)S(1)}, bf16[512,512]{1,0:T(8,128)(2,1)}, u32[]{:S(2)}) copy-start(bf16[512,512]{1,0:T(8,128)(2,1)} %cot_ref.3) | copy-start | bytes 1572868
  2.1 23.0 %collective-permute-start.2 = (f32[8,128]{1,0:T(8,128)S(1)}, f32[8,128]{1,0:T(8,128)S(1)}, u32[]{:S(2)}, u32[]{:S(2)}) collective-permute-start(f32[8,128]{1,0:T(8,128)S(1)} %get-tuple-element.20), channel_id=1, source_target_pairs={{0,256},{1,320},{2,352},{3,288},{4,384},{5,448},{6,480},{7,416},{8... | collective-permute-start | bytes 12296 | tf_op jit(solution)/shard_map/ppermute | solution.py:268
  17.7 6.3 %collective-permute-start = (bf16[128,512]{1,0:T(8,128)(2,1)S(1)}, bf16[128,512]{1,0:T(8,128)(2,1)S(1)}, u32[]{:S(2)}, u32[]{:S(2)}) collective-permute-start(bf16[128,512]{1,0:T(8,128)(2,1)S(1)} %get-tuple-element.18.own_far_ref), channel_id=1, source_target_pairs={{16,32},{32,16},{48,64},{64,48},{80,96},{96,80},{112,128},{128,112... | collective-permute-start | bytes 393224 | tf_op jit(solution)/shard_map/ppermute | solution.py:276
  19.7 4.4 %collective-permute-start.1 = (bf16[128,512]{1,0:T(8,128)(2,1)S(1)}, bf16[128,512]{1,0:T(8,128)(2,1)S(1)}, u32[]{:S(2)}, u32[]{:S(2)}) collective-permute-start(bf16[128,512]{1,0:T(8,128)(2,1)S(1)} %get-tuple-element.19.own_near_ref), channel_id=1, source_target_pairs={{0,16},{16,0},{32,48},{48,32},{64,80},{80,64},{96,112},{112,96},{1... | collective-permute-start | bytes 393224 | tf_op jit(solution)/shard_map/ppermute | solution.py:276
  40.7 14.9 %collective-permute-start.3 = (f32[16,128]{1,0:T(8,128)S(1)}, f32[16,128]{1,0:T(8,128)S(1)}, u32[]{:S(2)}, u32[]{:S(2)}) collective-permute-start(f32[16,128]{1,0:T(8,128)S(1)} %get-tuple-element.27), channel_id=1, source_target_pairs={{256,0},{320,1},{352,2},{288,3},{384,4},{448,5},{480,6},{416,7},{0... | collective-permute-start | bytes 24584 | tf_op jit(solution)/shard_map/ppermute | solution.py:268
  45.7 10.0 %copy-start.4 = (f32[16]{0:T(128)S(1)}, f32[16]{0:T(128)}, u32[]{:S(2)}) copy-start(f32[16]{0:T(128)} %param.11) | copy-start | bytes 196

commit v4 on v2

v4 whole, which is shorter than its diff:
```python
import math

import jax
import jax.numpy as jnp
from jax import lax
from jax.experimental import pallas as pl
from jax.experimental.pallas import tpu as pltpu
from jax.sharding import PartitionSpec as P

FILT = 128
GROUP = 16
LANES = 128
F32 = jnp.float32
BF16 = jnp.bfloat16
MIB = 1024 * 1024
NT = (((1,), (1,)), ((), ()))


def iota(shape, dim):
    return lax.broadcasted_iota(jnp.int32, shape, dim)


def flip_table():
    return ((iota((FILT, FILT), 0) + iota((FILT, FILT), 1)) % FILT == 0).astype(BF16)


def rounded_product(a, b):
    return (a.astype(F32) * b.astype(F32)).astype(BF16)


def front_kernel(key, value, query, cot, weight, rate, tail_ref, head_ref, taps_ref, *scratch):
    refs, sems = scratch[:-1], scratch[-1]
    tail = pl.ds(key.shape[0] - FILT, FILT)
    head = pl.ds(0, FILT)
    sources = [weight, rate, key.at[tail], value.at[tail], query.at[head], cot.at[head]]
    copies = [pltpu.make_async_copy(s, d, sems.at[i]) for i, (s, d) in enumerate(zip(sources, refs))]
    for copy in copies:
        copy.start()
    weight_ref, rate_ref = refs[:2]
    tap_count, group_count = weight.shape
    taps = (lax.axis_index("fsdp") * tap_count + iota((tap_count, group_count), 0)).astype(F32)
    taps_ref[...] = jnp.zeros_like(taps_ref)
    for copy in copies[:2]:
        copy.wait()
    decayed = weight_ref[...] * jnp.exp(-jnp.exp(rate_ref[...]) * taps)
    high = decayed.astype(BF16).astype(F32)
    taps_ref[:, :group_count] = high
    taps_ref[:, group_count : 2 * group_count] = decayed - high
    for copy in copies[2:]:
        copy.wait()
    key_ref, value_ref, query_ref, cot_ref = refs[2:]
    tail_ref[...] = rounded_product(key_ref[...], value_ref[...])
    head_ref[...] = rounded_product(cot_ref[...], query_ref[...])


def sums_kernel(key_ref, value_ref, query_ref, cot_ref, before_ref, sums_ref):
    blocks = key_ref.shape[0] // FILT
    groups = LANES // GROUP
    same = iota((FILT, FILT), 0) >= iota((FILT, FILT), 1)
    lane_group = (iota((FILT, blocks * LANES), 1) % LANES) // GROUP
    row = iota((groups * 8, LANES), 0) % 8
    sums = []
    for tile in range(key_ref.shape[1] // LANES):
        lanes = slice(tile * LANES, (tile + 1) * LANES)
        products = rounded_product(key_ref[:, lanes], value_ref[:, lanes])
        products = jnp.concatenate([before_ref[:, lanes], products], axis=0)
        grads = rounded_product(cot_ref[:, lanes], query_ref[:, lanes])
        left = jnp.concatenate([grads[b * FILT : (b + 1) * FILT] for b in range(blocks)], axis=1)
        right = jnp.concatenate([products[b * FILT : (b + 2) * FILT] for b in range(blocks)], axis=1)
        zero = jnp.zeros_like(left)
        stacked = jnp.concatenate([jnp.where(lane_group == g, left, zero) for g in range(groups)], axis=0)
        outer = lax.dot_general(stacked, right, NT, preferred_element_type=F32)
        squares = []
        for g in range(groups):
            rows = slice(g * FILT, (g + 1) * FILT)
            squares.append(jnp.where(same, outer[rows, FILT:], outer[rows, :FILT]))
        rolled = jnp.zeros((groups * 8, LANES), F32)
        for i in range(FILT // 8):
            part = jnp.concatenate([m[8 * i : 8 * i + 8] for m in squares], axis=0)
            rolled = rolled + (pltpu.roll(part, FILT - 8 * i, axis=1) if i else part)
        for step in (1, 2, 4):
            rolled = jnp.where((row & step) != 0, pltpu.roll(rolled, FILT - step, axis=1), rolled)
        sums.append(rolled.reshape(groups, 8, LANES).sum(axis=1))
    backwards = jnp.concatenate(sums, axis=0).astype(BF16)
    sums_ref[...] = jnp.dot(backwards, flip_table(), preferred_element_type=F32)


def message_kernel(sums_ref, taps_ref, out_ref):
    half = sums_ref.shape[0] // 2
    taps = taps_ref[...]
    halves = [
        jnp.concatenate([sums_ref[h * half : (h + 1) * half], taps], axis=0).astype(BF16) for h in range(2)
    ]
    for peer in range(out_ref.shape[0]):
        out_ref[peer] = halves[peer % 2]


LANDING = ((0, 2, 3, 1), (0, 1, 2, 3), (0, 1, 2, 3), (2, 0, 1, 3))
SIDE = 4


def landing(ctx, fsdp):
    column, half = ctx // 2, ctx % 2
    x, hi = fsdp // SIDE, fsdp % SIDE
    place = (x + 2) % SIDE * SIDE + LANDING[column % SIDE][hi]
    return place * 2 + half, column


def by_column(column, values):
    out = values[1]
    for q in (0, 3):
        out = jnp.where(column % SIDE == q, values[q], out)
    return out


def landed_piece(ctx, column):
    low = ctx // 2 % SIDE
    hi = jnp.int32(0)
    for z in range(SIDE):
        hi = jnp.where(low == z, by_column(column, [jnp.int32(LANDING[q].index(z)) for q in range(SIDE)]), hi)
    return (ctx // 8 + 2) % SIDE * SIDE + hi


def reduce_kernel(recv_ref, filt_ref, flipped_ref, home_ref):
    peers = recv_ref.shape[0]
    half = GROUP
    own, column = lax.axis_index("ctx"), lax.axis_index("fsdp")
    total = jnp.zeros((half, LANES), F32)
    landed = []
    for peer in range(peers):
        message = recv_ref[peer].astype(F32)
        total = total + message[:half]
        landed.append(message[half:])
    eye = (iota((2 * half, LANES), 0) == iota((2 * half, LANES), 1)).astype(BF16)
    turned = []
    for h in range(2):
        pieces = []
        for piece in range(peers // 2):
            x, hi = piece // SIDE, piece % SIDE
            places = [(x + 2) % SIDE * SIDE + LANDING[q][hi] for q in range(SIDE)]
            pieces.append(by_column(column, [landed[2 * place + h] for place in places]))
        pieces = jnp.concatenate(pieces, axis=0).astype(BF16)
        turned.append(lax.dot_general(eye, pieces, NT, preferred_element_type=F32))
    high = jnp.concatenate([t[:half] for t in turned], axis=0)
    filt_ref[...] = high
    flipped_ref[...] = jnp.dot(high.astype(BF16), flip_table(), preferred_element_type=F32)
    decayed = [t[:half] + t[half:] for t in turned]
    own_decayed = jnp.where(own % 2 == 0, decayed[0], decayed[1])
    lane = iota((half, LANES), 1)
    rate = jnp.sum(own_decayed * total * lane.astype(F32), axis=1, keepdims=True)
    tap_count = FILT * 2 // peers
    moved = pltpu.roll(total, (FILT - tap_count * landed_piece(own, column)) % FILT, axis=1)
    home_ref[...] = jnp.where(lane < tap_count, moved, rate)


def circulants(rows):
    return jnp.concatenate(
        [
            pltpu.roll(jnp.broadcast_to(rows[g : g + 1], (FILT, FILT)), 0, axis=1, stride=1, stride_axis=0)
            for g in range(rows.shape[0])
        ],
        axis=0,
    )


def banded_pair(rows, first, second):
    whole = circulants(rows)
    zero = jnp.zeros_like(whole)
    return jnp.concatenate([jnp.where(first, whole, zero), jnp.where(second, whole, zero)], axis=1).astype(BF16)


def apply_filters(band, padded, blocks):
    groups, step = LANES // GROUP, 32
    right = jnp.concatenate([padded[b * FILT : (b + 2) * FILT] for b in range(blocks)], axis=1)
    lane_group = iota((step, LANES), 1) // GROUP
    parts = [[] for _ in range(blocks)]
    for first in range(0, FILT, step):
        left = jnp.concatenate([band[g * FILT + first : g * FILT + first + step] for g in range(groups)], axis=0)
        wide = jnp.dot(left, right, preferred_element_type=F32)
        for b in range(blocks):
            lanes = slice(b * LANES, (b + 1) * LANES)
            kept = wide[:step, lanes]
            for g in range(1, groups):
                kept = jnp.where(lane_group == g, wide[g * step : (g + 1) * step, lanes], kept)
            parts[b].append(kept)
    return [jnp.concatenate(p, axis=0) for p in parts]


def outputs_kernel(
    key_ref, value_ref, query_ref, cot_ref, before_ref, after_ref, filt_ref, flipped_ref, *rest
):
    places, buffers, sems = rest[:4], rest[4:8], rest[8]
    blocks = key_ref.shape[0] // FILT
    groups = LANES // GROUP
    shape = (groups * FILT, FILT)
    row, col = iota(shape, 0) % FILT, iota(shape, 1)
    copies = []

    def send(index, tile):
        lanes = pl.ds(tile * LANES, LANES)
        copy = pltpu.make_async_copy(
            buffers[index].at[:, lanes], places[index].at[:, lanes], sems.at[len(copies)]
        )
        copy.start()
        copies.append(copy)

    for tile in range(key_ref.shape[1] // LANES):
        lanes = slice(tile * LANES, (tile + 1) * LANES)
        own = slice(tile * groups, (tile + 1) * groups)
        key, value = key_ref[:, lanes].astype(F32), value_ref[:, lanes].astype(F32)
        query, cot = query_ref[:, lanes].astype(F32), cot_ref[:, lanes].astype(F32)
        products = jnp.concatenate([before_ref[:, lanes], (key * value).astype(BF16)], axis=0)
        forward = banded_pair(flipped_ref[own], row < col, row >= col)
        for b, mixed in enumerate(apply_filters(forward, products, blocks)):
            rows = slice(b * FILT, (b + 1) * FILT)
            buffers[0][rows, lanes] = (query[rows] * mixed).astype(BF16)
            buffers[1][rows, lanes] = (cot[rows] * mixed).astype(BF16)
        send(0, tile)
        send(1, tile)
        grads = jnp.concatenate([(cot * query).astype(BF16), after_ref[:, lanes]], axis=0)
        backward = banded_pair(filt_ref[own], row <= col, row > col)
        for b, back in enumerate(apply_filters(backward, grads, blocks)):
            rows = slice(b * FILT, (b + 1) * FILT)
            buffers[2][rows, lanes] = (back * value[rows]).astype(BF16)
            buffers[3][rows, lanes] = (back * key[rows]).astype(BF16)
        send(2, tile)
        send(3, tile)
    for copy in copies:
        copy.wait()


def finish_kernel(home_ref, rate_ref, grad_filter_ref, grad_rate_ref, *, scale):
    tap_count, group_count = grad_filter_ref.shape
    turned = home_ref[...].T
    first_tap = lax.axis_index("fsdp") * tap_count
    taps = (first_tap + iota((tap_count, group_count), 0)).astype(F32)
    rates = jnp.exp(rate_ref[...])
    grad_filter_ref[...] = turned[:tap_count, :group_count] * jnp.exp(-rates * taps) * scale
    grad_rate_ref[...] = turned[tap_count : tap_count + 1, :group_count] * (-rates) * scale


def in_hbm(value):
    return pltpu.with_memory_space_constraint(value, pltpu.HBM)


def params(mib=24):
    return pltpu.CompilerParams(vmem_limit_bytes=mib * MIB)


def cost(us):
    return pl.CostEstimate(flops=int(us * 1e9), bytes_accessed=int(us * 3_000_000), transcendentals=0)


def moved_pieces(value, back):
    ctx, fsdp = lax.axis_size("ctx"), lax.axis_size("fsdp")
    pairs = []
    for c in range(ctx):
        for f in range(fsdp):
            there, column = landing(c, f)
            pairs.append((c * fsdp + f, there * fsdp + column))
    return lax.ppermute(value, ("ctx", "fsdp"), [(b, a) for a, b in pairs] if back else pairs)


def passed_along(value, by):
    peers = lax.axis_size("ctx")
    pairs = [(i, i + by) for i in range(peers) if 0 <= i + by < peers]
    return lax.ppermute(value, "ctx", pairs)


def per_device(query, key_in, value_in, cotangent, filter_weight, log_rate):
    tokens, channels = query.shape
    peers = lax.axis_size("ctx")
    groups = channels // GROUP
    scale = 1.0 / math.sqrt(tokens * peers * GROUP)
    rate_row = log_rate.reshape(1, -1)
    sds = jax.ShapeDtypeStruct
    tap_count, tap_groups = filter_weight.shape

    edge = (FILT, channels)
    anywhere = pl.BlockSpec(memory_space=pl.ANY)
    tail, head, taps = pl.pallas_call(
        front_kernel,
        in_specs=[anywhere] * 6,
        out_shape=[sds(edge, BF16), sds(edge, BF16), sds((tap_count, LANES), F32)],
        scratch_shapes=[pltpu.VMEM(filter_weight.shape, F32), pltpu.VMEM(rate_row.shape, F32)]
        + [pltpu.VMEM(edge, BF16)] * 4
        + [pltpu.SemaphoreType.DMA((6,))],
        compiler_params=params(),
    )(*(in_hbm(x) for x in (key_in, value_in, query, cotangent, filter_weight, rate_row)))
    taps_here = moved_pieces(taps, False)
    before = passed_along(tail, 1)
    after = passed_along(head, -1)

    sums = pl.pallas_call(
        sums_kernel,
        out_shape=sds((groups, LANES), F32),
        cost_estimate=cost(0.5),
        compiler_params=params(),
    )(key_in, value_in, query, cotangent, before)
    message = pl.pallas_call(
        message_kernel,
        out_shape=sds((peers, groups // 2 + tap_count, LANES), BF16),
        compiler_params=params(),
    )(sums, taps_here)
    received = lax.all_to_all(message, "ctx", 0, 0, tiled=True)
    filt, flipped, home = pl.pallas_call(
        reduce_kernel,
        out_shape=[sds((groups, LANES), F32), sds((groups, LANES), F32), sds((groups // 2, LANES), F32)],
        compiler_params=params(),
    )(received)
    home = moved_pieces(home, True)
    output, grad_query, grad_key, grad_value = pl.pallas_call(
        outputs_kernel,
        out_specs=[anywhere] * 4,
        out_shape=[sds((tokens, channels), BF16)] * 4,
        scratch_shapes=[pltpu.VMEM((tokens, channels), BF16)] * 4
        + [pltpu.SemaphoreType.DMA((4 * channels // LANES,))],
        compiler_params=params(),
    )(key_in, value_in, query, cotangent, before, after, filt, flipped)
    grad_filter, grad_rate = pl.pallas_call(
        lambda *refs: finish_kernel(*refs, scale=scale),
        out_shape=[sds(filter_weight.shape, F32), sds(rate_row.shape, F32)],
        compiler_params=params(),
    )(home, rate_row)
    return (output, grad_query, grad_key, grad_value, grad_filter, grad_rate.reshape(log_rate.shape))


def solution(mesh):
    specs = (P("ctx", "fsdp"),) * 4 + (P("fsdp", "ctx"), P("ctx"))
    return jax.shard_map(per_device, mesh=mesh, in_specs=specs, out_specs=specs, check_vma=False)
```

time: 58.3 us -> 53.5 us (0.918)
  starting transfers between devices: 42.5 us -> 39 us
  Pallas kernels: 10.9 us -> 8.07 us
  waiting for transfers between devices: 3.74 us -> 5.29 us
    pallas_call x3 -> x2, Pallas kernels: 7.35 us -> 5.13 us  [the longest x1 3.42 us: per_device(): pl.pallas_call(outputs_kernel, out_specs=[anywhere] * 4, out_shape=[sds((...]
    all_to_all x1, starting transfers between devices: 10.7 us -> 8.69 us  [per_device(): received = lax.all_to_all(message, 'ctx', 0, 0, tiled=True)]
    ppermute x2, starting transfers between devices: 5.92 us -> 4.67 us  [passed_along(): return lax.ppermute(value, 'ctx', pairs)]
    all_to_all x1, waiting for transfers between devices: 3.73 us -> 4.74 us  [per_device(): received = lax.all_to_all(message, 'ctx', 0, 0, tiled=True)]
    pallas_call x1, Pallas kernels: 2.02 us -> 1.38 us  [per_device(): pl.pallas_call(front_kernel, in_specs=[anywhere] * 6, out_shape=[sds(edge...]
  transfers between devices with their start and end apart: 5 -> 5, of which waited for: 1 -> 2; matrix products, arithmetic and copies ran while one was open for 0% -> 0% of each run, Pallas kernels for 13% -> 10%
where the time goes in v4:
time: 53.5 us; the launch traced here: 53.2 us
  starting transfers between devices  39 us (73%)
  Pallas kernels  8.07 us (15%)
  waiting for transfers between devices  5.29 us (10%)
  between operations  0.79 us (1%)
    ppermute x2, starting transfers between devices, moved_pieces(): lax.ppermute(value, ('ctx', 'fsdp'), [(b, a) for a, b in pairs] if back e...  25.7 us
    all_to_all x1, starting transfers between devices, per_device(): received = lax.all_to_all(message, 'ctx', 0, 0, tiled=True)  8.69 us
    all_to_all x1, waiting for transfers between devices, per_device(): received = lax.all_to_all(message, 'ctx', 0, 0, tiled=True)  4.74 us
    ppermute x2, starting transfers between devices, passed_along(): return lax.ppermute(value, 'ctx', pairs)  4.67 us
    pallas_call x1, Pallas kernels, per_device(): pl.pallas_call(outputs_kernel, out_specs=[anywhere] * 4, out_shape=[sds((...  3.42 us
    pallas_call x1, Pallas kernels, per_device(): pl.pallas_call(sums_kernel, out_shape=sds((groups, LANES), F32), cost_est...  1.7 us
    pallas_call x1, Pallas kernels, per_device(): pl.pallas_call(front_kernel, in_specs=[anywhere] * 6, out_shape=[sds(edge...  1.38 us
  transfers between devices with their start and end apart: 5, of which 2 were waited for; matrix products, arithmetic and copies ran while one was open for 0% of the time, Pallas kernels for 10%

profile of v4, /device:TPU:105, one launch (start us, length us, event | category | flops | bytes accessed | tf_op | source)
XLA Modules:
  0.0 53.2 jit_solution(10678465587661412742)
XLA Ops:
  0.6 0.0 copy-start
  0.6 0.0 copy-start.1
  0.7 0.0 copy-start.2
  0.7 0.0 copy-start.3
  0.7 1.4 %shard_map.109 = (bf16[128,512]{1,0:T(8,128)(2,1)S(1)}, bf16[128,512]{1,0:T(8,128)(2,1)S(1)}, f32[8,128]{1,0:T(8,128)S(1)}) custom-call(bf16[512,512]{1,0:T(8,128)(2,1)} %key_ref.3, bf16[512,512]{1,0:T(8,128)(2,1)} %value_ref.3, bf16[512,512]{1,0:T(8,128)(2,1)} %query_ref.3, bf16[512,512]{1,0:T(8,128)(2,1)} %cot_ref.3, f32[8,16]{1,0:T(8,128)} %weight.1, ...), custom_call_target="tpu_custom_call" | custom-call | tf_op jit(solution)/shard_map/pallas_call | solution.py:281
  2.1 2.4 %collective-permute-start = (bf16[128,512]{1,0:T(8,128)(2,1)S(1)}, bf16[128,512]{1,0:T(8,128)(2,1)S(1)}, u32[]{:S(2)}, u32[]{:S(2)}) collective-permute-start(bf16[128,512]{1,0:T(8,128)(2,1)S(1)} %get-tuple-element.18), channel_id=1, source_target_pairs={{0,16},{16,32},{32,48},{48,64},{64,80},{80,96},{96,112},{112,128},... | collective-permute-start | bytes 393224 | tf_op jit(solution)/shard_map/ppermute | solution.py:267
  4.5 12.9 %collective-permute-start.2 = (f32[8,128]{1,0:T(8,128)S(1)}, f32[8,128]{1,0:T(8,128)S(1)}, u32[]{:S(2)}, u32[]{:S(2)}) collective-permute-start(f32[8,128]{1,0:T(8,128)S(1)} %get-tuple-element.20), channel_id=1, source_target_pairs={{0,256},{1,320},{2,352},{3,288},{4,384},{5,448},{6,480},{7,416},{8... | collective-permute-start | bytes 12296 | tf_op jit(solution)/shard_map/ppermute | solution.py:261
  17.4 0.0 collective-permute-done.before_ref
  17.4 0.0 copy-done
  17.4 0.0 copy-done.1
  17.5 0.0 copy-done.2
  17.5 1.7 %shard_map.110.sums_ref = f32[32,128]{1,0:T(8,128)S(1)} custom-call(bf16[512,512]{1,0:T(8,128)(2,1)S(1)} %copy-done, bf16[512,512]{1,0:T(8,128)(2,1)S(1)} %copy-done.1, bf16[512,512]{1,0:T(8,128)(2,1)S(1)} %copy-done.2, bf16[512,512]{1,0:T(8,128)(2,1)S(1)} %copy-done.3, bf16[128,512]{1,0:T(8,128)(2,1)S(1)} %collective-permute-done.before_ref), custom_call_target="tpu_custom_call" | custom-call | flops 500000000 | bytes 1500000 | tf_op jit(solution)/shard_map/pallas_call | solution.py:294
  19.2 0.5 %collective-permute-done.2.taps_ref = f32[8,128]{1,0:T(8,128)S(1)} collective-permute-done((f32[8,128]{1,0:T(8,128)S(1)}, f32[8,128]{1,0:T(8,128)S(1)}, u32[]{:S(2)}, u32[]{:S(2)}) %collective-permute-start.2) | collective-permute-done | bytes 4128 | tf_op jit(solution)/shard_map/ppermute | solution.py:261
  19.7 0.7 %shard_map.111 = bf16[32,24,128]{2,1,0:T(8,128)(2,1)} custom-call(f32[32,128]{1,0:T(8,128)S(1)} %shard_map.110.sums_ref, f32[8,128]{1,0:T(8,128)S(1)} %collective-permute-done.2.taps_ref), custom_call_target="tpu_custom_call" | custom-call | tf_op jit(solution)/shard_map/pallas_call | solution.py:300
  20.4 8.7 %all-to-all-start = ((bf16[32,24,128]{2,1,0:T(8,128)(2,1)}), bf16[32,24,128]{2,1,0:T(8,128)(2,1)S(1)}, u32[]{:S(2)}, u32[]{:S(2)}) async-start(bf16[32,24,128]{2,1,0:T(8,128)(2,1)} %shard_map.111), calls=%async_computation | async-start | bytes 393216 | tf_op jit(solution)/shard_map/all_to_all | solution.py:305
  29.1 2.3 %collective-permute-start.1 = (bf16[128,512]{1,0:T(8,128)(2,1)S(1)}, bf16[128,512]{1,0:T(8,128)(2,1)S(1)}, u32[]{:S(2)}, u32[]{:S(2)}) collective-permute-start(bf16[128,512]{1,0:T(8,128)(2,1)S(1)} %get-tuple-element.19), channel_id=1, source_target_pairs={{16,0},{32,16},{48,32},{64,48},{80,64},{96,80},{112,96},{128,112},... | collective-permute-start | bytes 393224 | tf_op jit(solution)/shard_map/ppermute | solution.py:267
  31.4 4.7 %all-to-all-done.recv_ref = bf16[32,24,128]{2,1,0:T(8,128)(2,1)S(1)} async-done(((bf16[32,24,128]{2,1,0:T(8,128)(2,1)}), bf16[32,24,128]{2,1,0:T(8,128)(2,1)S(1)}, u32[]{:S(2)}, u32[]{:S(2)}) %all-to-all-start) | async-done | bytes 196640 | tf_op jit(solution)/shard_map/all_to_all | solution.py:305
  36.1 0.2 shard_map.112
  36.3 12.7 %collective-permute-start.3 = (f32[16,128]{1,0:T(8,128)S(1)}, f32[16,128]{1,0:T(8,128)S(1)}, u32[]{:S(2)}, u32[]{:S(2)}) collective-permute-start(f32[16,128]{1,0:T(8,128)S(1)} %get-tuple-element.27), channel_id=1, source_target_pairs={{256,0},{320,1},{352,2},{288,3},{384,4},{448,5},{480,6},{416,7},{0... | collective-permute-start | bytes 24584 | tf_op jit(solution)/shard_map/ppermute | solution.py:261
  49.1 0.0 collective-permute-done.1.after_ref
  49.1 0.0 copy-start.4
  49.1 3.4 %shard_map.113 = (bf16[512,512]{1,0:T(8,128)(2,1)}, bf16[512,512]{1,0:T(8,128)(2,1)}, bf16[512,512]{1,0:T(8,128)(2,1)}, bf16[512,512]{1,0:T(8,128)(2,1)}) custom-call(bf16[512,512]{1,0:T(8,128)(2,1)S(1)} %copy-done, bf16[512,512]{1,0:T(8,128)(2,1)S(1)} %copy-done.1, bf16[512,512]{1,0:T(8,128)(2,1)S(1)} %copy-done.2, bf16[512,512]{1,0:T(8,128)(2,1)S(1)} %copy-done.3, ...), custom_call_target="tpu_custom_call" | custom-call | tf_op jit(solution)/shard_map/pallas_call | solution.py:312
  52.5 0.0 collective-permute-done.3.refs_0_
  52.5 0.7 %shard_map.114 = (f32[8,16]{1,0:T(8,128)}, f32[1,16]{1,0:T(1,128)}) custom-call(f32[16,128]{1,0:T(8,128)S(1)} %collective-permute-done.3.refs_0_, f32[1,16]{1,0:T(1,128)S(1)} %bitcast.3), custom_call_target="tpu_custom_call" | custom-call | tf_op jit(solution)/shard_map/pallas_call | solution.py:320
  (2 shorter events, 0.0 us)
Async XLA Ops:
  0.6 16.8 %copy-start = (bf16[512,512]{1,0:T(8,128)(2,1)S(1)}, bf16[512,512]{1,0:T(8,128)(2,1)}, u32[]{:S(2)}) copy-start(bf16[512,512]{1,0:T(8,128)(2,1)} %key_ref.3) | copy-start | bytes 1572868
  0.6 16.8 %copy-start.1 = (bf16[512,512]{1,0:T(8,128)(2,1)S(1)}, bf16[512,512]{1,0:T(8,128)(2,1)}, u32[]{:S(2)}) copy-start(bf16[512,512]{1,0:T(8,128)(2,1)} %value_ref.3) | copy-start | bytes 1572868
  0.7 16.8 %copy-start.2 = (bf16[512,512]{1,0:T(8,128)(2,1)S(1)}, bf16[512,512]{1,0:T(8,128)(2,1)}, u32[]{:S(2)}) copy-start(bf16[512,512]{1,0:T(8,128)(2,1)} %query_ref.3) | copy-start | bytes 1572868
  0.7 16.8 %copy-start.3 = (bf16[512,512]{1,0:T(8,128)(2,1)S(1)}, bf16[512,512]{1,0:T(8,128)(2,1)}, u32[]{:S(2)}) copy-start(bf16[512,512]{1,0:T(8,128)(2,1)} %cot_ref.3) | copy-start | bytes 1572868
  2.1 15.4 %collective-permute-start = (bf16[128,512]{1,0:T(8,128)(2,1)S(1)}, bf16[128,512]{1,0:T(8,128)(2,1)S(1)}, u32[]{:S(2)}, u32[]{:S(2)}) collective-permute-start(bf16[128,512]{1,0:T(8,128)(2,1)S(1)} %get-tuple-element.18), channel_id=1, source_target_pairs={{0,16},{16,32},{32,48},{48,64},{64,80},{80,96},{96,112},{112,128},... | collective-permute-start | bytes 393224 | tf_op jit(solution)/shard_map/ppermute | solution.py:267
  4.5 15.3 %collective-permute-start.2 = (f32[8,128]{1,0:T(8,128)S(1)}, f32[8,128]{1,0:T(8,128)S(1)}, u32[]{:S(2)}, u32[]{:S(2)}) collective-permute-start(f32[8,128]{1,0:T(8,128)S(1)} %get-tuple-element.20), channel_id=1, source_target_pairs={{0,256},{1,320},{2,352},{3,288},{4,384},{5,448},{6,480},{7,416},{8... | collective-permute-start | bytes 12296 | tf_op jit(solution)/shard_map/ppermute | solution.py:261
  20.4 15.7 %all-to-all-start = ((bf16[32,24,128]{2,1,0:T(8,128)(2,1)}), bf16[32,24,128]{2,1,0:T(8,128)(2,1)S(1)}, u32[]{:S(2)}, u32[]{:S(2)}) async-start(bf16[32,24,128]{2,1,0:T(8,128)(2,1)} %shard_map.111), calls=%async_computation | async-start | bytes 393216 | tf_op jit(solution)/shard_map/all_to_all | solution.py:305
  29.1 19.9 %collective-permute-start.1 = (bf16[128,512]{1,0:T(8,128)(2,1)S(1)}, bf16[128,512]{1,0:T(8,128)(2,1)S(1)}, u32[]{:S(2)}, u32[]{:S(2)}) collective-permute-start(bf16[128,512]{1,0:T(8,128)(2,1)S(1)} %get-tuple-element.19), channel_id=1, source_target_pairs={{16,0},{32,16},{48,32},{64,48},{80,64},{96,80},{112,96},{128,112},... | collective-permute-start | bytes 393224 | tf_op jit(solution)/shard_map/ppermute | solution.py:267
  36.3 16.2 %collective-permute-start.3 = (f32[16,128]{1,0:T(8,128)S(1)}, f32[16,128]{1,0:T(8,128)S(1)}, u32[]{:S(2)}, u32[]{:S(2)}) collective-permute-start(f32[16,128]{1,0:T(8,128)S(1)} %get-tuple-element.27), channel_id=1, source_target_pairs={{256,0},{320,1},{352,2},{288,3},{384,4},{448,5},{480,6},{416,7},{0... | collective-permute-start | bytes 24584 | tf_op jit(solution)/shard_map/ppermute | solution.py:261
  49.1 3.5 %copy-start.4 = (f32[16]{0:T(128)S(1)}, f32[16]{0:T(128)}, u32[]{:S(2)}) copy-start(f32[16]{0:T(128)} %param.11) | copy-start | bytes 196

commit v5 on v4

--- a/solution.py
+++ b/solution.py
@@ -28,11 +28,10 @@
     return (a.astype(F32) * b.astype(F32)).astype(BF16)
 
 
-def front_kernel(key, value, query, cot, weight, rate, tail_ref, head_ref, taps_ref, *scratch):
+def front_kernel(key, value, query, cot, weight, rate, tail_ref, late_tail_ref, taps_ref, *scratch):
     refs, sems = scratch[:-1], scratch[-1]
     tail = pl.ds(key.shape[0] - FILT, FILT)
-    head = pl.ds(0, FILT)
-    sources = [weight, rate, key.at[tail], value.at[tail], query.at[head], cot.at[head]]
+    sources = [weight, rate, key.at[tail], value.at[tail]]
     copies = [pltpu.make_async_copy(s, d, sems.at[i]) for i, (s, d) in enumerate(zip(sources, refs))]
     for copy in copies:
         copy.start()
@@ -48,41 +47,91 @@
     taps_ref[:, group_count : 2 * group_count] = decayed - high
     for copy in copies[2:]:
         copy.wait()
-    key_ref, value_ref, query_ref, cot_ref = refs[2:]
-    tail_ref[...] = rounded_product(key_ref[...], value_ref[...])
-    head_ref[...] = rounded_product(cot_ref[...], query_ref[...])
-
-
-def sums_kernel(key_ref, value_ref, query_ref, cot_ref, before_ref, sums_ref):
+    products = rounded_product(refs[2][...], refs[3][...])
+    tail_ref[...] = products
+    late_tail_ref[...] = products
+
+
+LANDING = ((0, 2, 3, 1), (0, 1, 2, 3), (0, 1, 2, 3), (2, 0, 1, 3))
+SIDE = 4
+
+
+def is_late():
+    return lax.axis_index("fsdp") % SIDE != 0
+
+
+HALF = LANES // 2
+
+
+def packed_halves(blocks_list):
+    low = iota((FILT, LANES), 1) < HALF
+    turned = [pltpu.roll(x, HALF, axis=1) for x in blocks_list]
+
+    def pair(half, i, j):
+        first, second = (blocks_list[i], turned[j]) if half == 0 else (turned[i], blocks_list[j])
+        return jnp.where(low, first, second)
+
+    return pair
+
+
+def diagonal_sums(left, right, period):
+    step, groups = FILT // 2, period // GROUP
+    lane_group = (iota((step, left.shape[1]), 1) % period) // GROUP
+    zero = jnp.zeros((step, left.shape[1]), BF16)
+    total = jnp.zeros((groups * 8, LANES), F32)
+    for first in range(0, FILT, step):
+        rows = left[first : first + step]
+        stacked = jnp.concatenate([jnp.where(lane_group == g, rows, zero) for g in range(groups)], axis=0)
+        outer = lax.dot_general(stacked, right, NT, preferred_element_type=F32)
+        for i in range(first, first + step, 8):
+            same = iota((8, FILT), 0) + i >= iota((8, FILT), 1)
+            parts = []
+            for g in range(groups):
+                row = slice(g * step + i - first, g * step + i - first + 8)
+                before = outer[row, :FILT]
+                own = outer[row, FILT:] if right.shape[0] > FILT else jnp.zeros_like(before)
+                parts.append(jnp.where(same, own, before))
+            part = jnp.concatenate(parts, axis=0)
+            total = total + (pltpu.roll(part, FILT - i, axis=1) if i else part)
+    row = iota(total.shape, 0) % 8
+    for step in (1, 2, 4):
+        total = jnp.where((row & step) != 0, pltpu.roll(total, FILT - step, axis=1), total)
+    return total.reshape(groups, 8, LANES).sum(axis=1)
+
+
+def sums_kernel(key_ref, value_ref, query_ref, cot_ref, before_ref, sums_ref, head_ref):
     blocks = key_ref.shape[0] // FILT
-    groups = LANES // GROUP
-    same = iota((FILT, FILT), 0) >= iota((FILT, FILT), 1)
-    lane_group = (iota((FILT, blocks * LANES), 1) % LANES) // GROUP
-    row = iota((groups * 8, LANES), 0) % 8
     sums = []
     for tile in range(key_ref.shape[1] // LANES):
         lanes = slice(tile * LANES, (tile + 1) * LANES)
         products = rounded_product(key_ref[:, lanes], value_ref[:, lanes])
-        products = jnp.concatenate([before_ref[:, lanes], products], axis=0)
         grads = rounded_product(cot_ref[:, lanes], query_ref[:, lanes])
-        left = jnp.concatenate([grads[b * FILT : (b + 1) * FILT] for b in range(blocks)], axis=1)
-        right = jnp.concatenate([products[b * FILT : (b + 2) * FILT] for b in range(blocks)], axis=1)
-        zero = jnp.zeros_like(left)
-        stacked = jnp.concatenate([jnp.where(lane_group == g, left, zero) for g in range(groups)], axis=0)
-        outer = lax.dot_general(stacked, right, NT, preferred_element_type=F32)
-        squares = []
-        for g in range(groups):
-            rows = slice(g * FILT, (g + 1) * FILT)
-            squares.append(jnp.where(same, outer[rows, FILT:], outer[rows, :FILT]))
-        rolled = jnp.zeros((groups * 8, LANES), F32)
-        for i in range(FILT // 8):
-            part = jnp.concatenate([m[8 * i : 8 * i + 8] for m in squares], axis=0)
-            rolled = rolled + (pltpu.roll(part, FILT - 8 * i, axis=1) if i else part)
-        for step in (1, 2, 4):
-            rolled = jnp.where((row & step) != 0, pltpu.roll(rolled, FILT - step, axis=1), rolled)
-        sums.append(rolled.reshape(groups, 8, LANES).sum(axis=1))
-    backwards = jnp.concatenate(sums, axis=0).astype(BF16)
-    sums_ref[...] = jnp.dot(backwards, flip_table(), preferred_element_type=F32)
+        head_ref[:, lanes] = grads[:FILT]
+        ours = packed_halves([grads[b * FILT : (b + 1) * FILT] for b in range(blocks)])
+        theirs = packed_halves(
+            [before_ref[:, lanes]] + [products[b * FILT : (b + 1) * FILT] for b in range(blocks)]
+        )
+        pairs = range(0, blocks, 2)
+        for half in range(2):
+            left = jnp.concatenate([ours(half, b, b + 1) for b in pairs], axis=1)
+            earlier = jnp.concatenate([theirs(half, b, b + 1) for b in pairs], axis=1)
+            own = jnp.concatenate([theirs(half, b + 1, b + 2) for b in pairs], axis=1)
+            sums.append(diagonal_sums(left, jnp.concatenate([earlier, own], axis=0), HALF))
+    sums_ref[...] = jnp.concatenate(sums, axis=0)
+
+
+def ordered_kernel(sums_ref, before_ref, head_ref, out_ref, total_ref):
+    total_ref[...] = sums_ref[...]
+
+    @pl.when(is_late())
+    def _():
+        groups = LANES // GROUP
+        for tile in range(head_ref.shape[1] // LANES):
+            lanes = slice(tile * LANES, (tile + 1) * LANES)
+            rows = slice(tile * groups, (tile + 1) * groups)
+            total_ref[rows] = total_ref[rows] + diagonal_sums(head_ref[:, lanes], before_ref[:, lanes], LANES)
+
+    out_ref[...] = jnp.dot(total_ref[...].astype(BF16), flip_table(), preferred_element_type=F32)
 
 
 def message_kernel(sums_ref, taps_ref, out_ref):
@@ -93,10 +142,6 @@
     ]
     for peer in range(out_ref.shape[0]):
         out_ref[peer] = halves[peer % 2]
-
-
-LANDING = ((0, 2, 3, 1), (0, 1, 2, 3), (0, 1, 2, 3), (2, 0, 1, 3))
-SIDE = 4
 
 
 def landing(ctx, fsdp):
@@ -187,7 +232,7 @@
 
 
 def outputs_kernel(
-    key_ref, value_ref, query_ref, cot_ref, before_ref, after_ref, filt_ref, flipped_ref, *rest
+    key_ref, value_ref, query_ref, cot_ref, early_ref, late_ref, after_ref, filt_ref, flipped_ref, *rest
 ):
     places, buffers, sems = rest[:4], rest[4:8], rest[8]
     blocks = key_ref.shape[0] // FILT
@@ -209,7 +254,8 @@
         own = slice(tile * groups, (tile + 1) * groups)
         key, value = key_ref[:, lanes].astype(F32), value_ref[:, lanes].astype(F32)
         query, cot = query_ref[:, lanes].astype(F32), cot_ref[:, lanes].astype(F32)
-        products = jnp.concatenate([before_ref[:, lanes], (key * value).astype(BF16)], axis=0)
+        before = jnp.where(is_late(), late_ref[:, lanes], early_ref[:, lanes])
+        products = jnp.concatenate([before, (key * value).astype(BF16)], axis=0)
         forward = banded_pair(flipped_ref[own], row < col, row >= col)
         for b, mixed in enumerate(apply_filters(forward, products, blocks)):
             rows = slice(b * FILT, (b + 1) * FILT)
@@ -261,10 +307,13 @@
     return lax.ppermute(value, ("ctx", "fsdp"), [(b, a) for a, b in pairs] if back else pairs)
 
 
-def passed_along(value, by):
-    peers = lax.axis_size("ctx")
-    pairs = [(i, i + by) for i in range(peers) if 0 <= i + by < peers]
-    return lax.ppermute(value, "ctx", pairs)
+def passed_along(value, by, chosen=lambda column: True):
+    ctx, fsdp = lax.axis_size("ctx"), lax.axis_size("fsdp")
+    pairs = [
+        (c * fsdp + f, (c + by) * fsdp + f)
+        for c in range(ctx) for f in range(fsdp) if 0 <= c + by < ctx and chosen(f)
+    ]
+    return lax.ppermute(value, ("ctx", "fsdp"), pairs)
 
 
 def per_device(query, key_in, value_in, cotangent, filter_weight, log_rate):
@@ -278,25 +327,32 @@
 
     edge = (FILT, channels)
     anywhere = pl.BlockSpec(memory_space=pl.ANY)
-    tail, head, taps = pl.pallas_call(
+    tail, late_tail, taps = pl.pallas_call(
         front_kernel,
         in_specs=[anywhere] * 6,
-        out_shape=[sds(edge, BF16), sds(edge, BF16), sds((tap_count, LANES), F32)],
+        out_shape=[sds(edge, BF16)] * 2 + [sds((tap_count, LANES), F32)],
         scratch_shapes=[pltpu.VMEM(filter_weight.shape, F32), pltpu.VMEM(rate_row.shape, F32)]
-        + [pltpu.VMEM(edge, BF16)] * 4
-        + [pltpu.SemaphoreType.DMA((6,))],
+        + [pltpu.VMEM(edge, BF16)] * 2
+        + [pltpu.SemaphoreType.DMA((4,))],
         compiler_params=params(),
     )(*(in_hbm(x) for x in (key_in, value_in, query, cotangent, filter_weight, rate_row)))
     taps_here = moved_pieces(taps, False)
-    before = passed_along(tail, 1)
+    early = passed_along(tail, 1, lambda f: f % SIDE == 0)
+    late = passed_along(late_tail, 1, lambda f: f % SIDE != 0)
+
+    sums, head = pl.pallas_call(
+        sums_kernel,
+        out_shape=[sds((groups, LANES), F32), sds(edge, BF16)],
+        cost_estimate=cost(3),
+        compiler_params=params(),
+    )(key_in, value_in, query, cotangent, early)
     after = passed_along(head, -1)
-
     sums = pl.pallas_call(
-        sums_kernel,
+        ordered_kernel,
         out_shape=sds((groups, LANES), F32),
-        cost_estimate=cost(0.5),
-        compiler_params=params(),
-    )(key_in, value_in, query, cotangent, before)
+        scratch_shapes=[pltpu.VMEM((groups, LANES), F32)],
+        compiler_params=params(),
+    )(sums, late, head)
     message = pl.pallas_call(
         message_kernel,
         out_shape=sds((peers, groups // 2 + tap_count, LANES), BF16),
@@ -316,7 +372,7 @@
         scratch_shapes=[pltpu.VMEM((tokens, channels), BF16)] * 4
         + [pltpu.SemaphoreType.DMA((4 * channels // LANES,))],
         compiler_params=params(),
-    )(key_in, value_in, query, cotangent, before, after, filt, flipped)
+    )(key_in, value_in, query, cotangent, early, late, after, filt, flipped)
     grad_filter, grad_rate = pl.pallas_call(
         lambda *refs: finish_kernel(*refs, scale=scale),
         out_shape=[sds(filter_weight.shape, F32), sds(rate_row.shape, F32)],

time: 53.5 us -> 52.2 us (0.976)
  the two profiles are of different devices: /device:TPU:105 before, /device:TPU:64 now
where the time goes in v5:
time: 52.2 us; the launch traced here: 51.9 us
  starting transfers between devices  35.9 us (69%)
  Pallas kernels  8.01 us (15%)
  waiting for transfers between devices  7.22 us (14%)
  between operations  0.8 us (2%)
    ppermute x2, starting transfers between devices, moved_pieces(): lax.ppermute(value, ('ctx', 'fsdp'), [(b, a) for a, b in pairs] if back e...  24.3 us
    all_to_all x1, starting transfers between devices, per_device(): received = lax.all_to_all(message, 'ctx', 0, 0, tiled=True)  6.82 us
    all_to_all x1, waiting for transfers between devices, per_device(): received = lax.all_to_all(message, 'ctx', 0, 0, tiled=True)  5.65 us
    ppermute x3, starting transfers between devices, passed_along(): return lax.ppermute(value, ('ctx', 'fsdp'), pairs)  4.81 us
    pallas_call x1, Pallas kernels, per_device(): pl.pallas_call(outputs_kernel, out_specs=[anywhere] * 4, out_shape=[sds((...  3.46 us
    pallas_call x1, Pallas kernels, per_device(): pl.pallas_call(sums_kernel, out_shape=[sds((groups, LANES), F32), sds(edg...  1.62 us
    ppermute x2, waiting for transfers between devices, moved_pieces(): lax.ppermute(value, ('ctx', 'fsdp'), [(b, a) for a, b in pairs] if back e...  1.57 us
    pallas_call x1, Pallas kernels, per_device(): pl.pallas_call(front_kernel, in_specs=[anywhere] * 6, out_shape=[sds(edge...  1.21 us
  transfers between devices with their start and end apart: 6, of which 2 were waited for; matrix products, arithmetic and copies ran while one was open for 0% of the time, Pallas kernels for 10%

profile of v5, /device:TPU:64, one launch (start us, length us, event | category | flops | bytes accessed | tf_op | source)
XLA Modules:
  0.0 51.9 jit_solution(2666694685176979304)
XLA Ops:
  0.6 0.0 copy-start
  0.6 0.0 copy-start.1
  0.7 0.0 copy-start.2
  0.7 0.0 copy-start.3
  0.7 1.2 %shard_map.109 = (bf16[128,512]{1,0:T(8,128)(2,1)S(1)}, bf16[128,512]{1,0:T(8,128)(2,1)S(1)}, f32[8,128]{1,0:T(8,128)S(1)}) custom-call(bf16[512,512]{1,0:T(8,128)(2,1)} %key_ref.3, bf16[512,512]{1,0:T(8,128)(2,1)} %value_ref.3, bf16[512,512]{1,0:T(8,128)(2,1)} %query_ref.3, bf16[512,512]{1,0:T(8,128)(2,1)} %cot_ref.3, f32[8,16]{1,0:T(8,128)} %weight.1, ...), custom_call_target="tpu_custom_call" | custom-call | tf_op jit(solution)/shard_map/pallas_call | solution.py:330
  1.9 1.9 %collective-permute-start = (bf16[128,512]{1,0:T(8,128)(2,1)S(1)}, bf16[128,512]{1,0:T(8,128)(2,1)S(1)}, u32[]{:S(2)}, u32[]{:S(2)}) collective-permute-start(bf16[128,512]{1,0:T(8,128)(2,1)S(1)} %get-tuple-element.20), channel_id=1, source_target_pairs={{0,16},{4,20},{8,24},{12,28},{16,32},{20,36},{24,40},{28,44},{32,4... | collective-permute-start | bytes 393224 | tf_op jit(solution)/shard_map/ppermute | solution.py:316
  3.8 14.4 %collective-permute-start.3 = (f32[8,128]{1,0:T(8,128)S(1)}, f32[8,128]{1,0:T(8,128)S(1)}, u32[]{:S(2)}, u32[]{:S(2)}) collective-permute-start(f32[8,128]{1,0:T(8,128)S(1)} %get-tuple-element.24), channel_id=1, source_target_pairs={{0,256},{1,320},{2,352},{3,288},{4,384},{5,448},{6,480},{7,416},{8... | collective-permute-start | bytes 12296 | tf_op jit(solution)/shard_map/ppermute | solution.py:307
  18.2 0.7 %collective-permute-start.1 = (bf16[128,512]{1,0:T(8,128)(2,1)S(1)}, bf16[128,512]{1,0:T(8,128)(2,1)S(1)}, u32[]{:S(2)}, u32[]{:S(2)}) collective-permute-start(bf16[128,512]{1,0:T(8,128)(2,1)S(1)} %get-tuple-element.21), channel_id=1, source_target_pairs={{1,17},{2,18},{3,19},{5,21},{6,22},{7,23},{9,25},{10,26},{11,27},{... | collective-permute-start | bytes 393224 | tf_op jit(solution)/shard_map/ppermute | solution.py:316
  18.9 0.0 collective-permute-done.before_ref.early_ref
  18.9 1.6 %shard_map.110 = (f32[32,128]{1,0:T(8,128)S(1)}, bf16[128,512]{1,0:T(8,128)(2,1)S(1)}) custom-call(bf16[512,512]{1,0:T(8,128)(2,1)S(1)} %copy-done, bf16[512,512]{1,0:T(8,128)(2,1)S(1)} %copy-done.1, bf16[512,512]{1,0:T(8,128)(2,1)S(1)} %copy-done.2, bf16[512,512]{1,0:T(8,128)(2,1)S(1)} %copy-done.3, ...), custom_call_target="tpu_custom_call" | custom-call | flops 3000000000 | bytes 9000000 | tf_op jit(solution)/shard_map/pallas_call | solution.py:343
  20.6 0.0 collective-permute-done.1.before_ref.late_ref
  20.6 0.1 shard_map.111.sums_ref
  20.7 0.0 collective-permute-done.3.taps_ref
  20.7 0.7 %shard_map.112 = bf16[32,24,128]{2,1,0:T(8,128)(2,1)} custom-call(f32[32,128]{1,0:T(8,128)S(1)} %shard_map.111.sums_ref, f32[8,128]{1,0:T(8,128)S(1)} %collective-permute-done.3.taps_ref), custom_call_target="tpu_custom_call" | custom-call | tf_op jit(solution)/shard_map/pallas_call | solution.py:356
  21.4 6.8 %all-to-all-start = ((bf16[32,24,128]{2,1,0:T(8,128)(2,1)}), bf16[32,24,128]{2,1,0:T(8,128)(2,1)S(1)}, u32[]{:S(2)}, u32[]{:S(2)}) async-start(bf16[32,24,128]{2,1,0:T(8,128)(2,1)} %shard_map.112), calls=%async_computation | async-start | bytes 393216 | tf_op jit(solution)/shard_map/all_to_all | solution.py:361
  28.3 2.2 %collective-permute-start.2 = (bf16[128,512]{1,0:T(8,128)(2,1)S(1)}, bf16[128,512]{1,0:T(8,128)(2,1)S(1)}, u32[]{:S(2)}, u32[]{:S(2)}) collective-permute-start(bf16[128,512]{1,0:T(8,128)(2,1)S(1)} %get-tuple-element.22.head_ref), channel_id=1, source_target_pairs={{16,0},{17,1},{18,2},{19,3},{20,4},{21,5},{22,6},{23,7},{24,8},{25... | collective-permute-start | bytes 393224 | tf_op jit(solution)/shard_map/ppermute | solution.py:316
  30.5 5.6 %all-to-all-done.recv_ref = bf16[32,24,128]{2,1,0:T(8,128)(2,1)S(1)} async-done(((bf16[32,24,128]{2,1,0:T(8,128)(2,1)}), bf16[32,24,128]{2,1,0:T(8,128)(2,1)S(1)}, u32[]{:S(2)}, u32[]{:S(2)}) %all-to-all-start) | async-done | bytes 196640 | tf_op jit(solution)/shard_map/all_to_all | solution.py:361
  36.1 0.2 shard_map.113
  36.4 9.9 %collective-permute-start.4 = (f32[16,128]{1,0:T(8,128)S(1)}, f32[16,128]{1,0:T(8,128)S(1)}, u32[]{:S(2)}, u32[]{:S(2)}) collective-permute-start(f32[16,128]{1,0:T(8,128)S(1)} %get-tuple-element.31), channel_id=1, source_target_pairs={{256,0},{320,1},{352,2},{288,3},{384,4},{448,5},{480,6},{416,7},{0... | collective-permute-start | bytes 24584 | tf_op jit(solution)/shard_map/ppermute | solution.py:307
  46.2 0.0 collective-permute-done.2.after_ref
  46.2 0.0 copy-start.4
  46.2 3.5 %shard_map.114 = (bf16[512,512]{1,0:T(8,128)(2,1)}, bf16[512,512]{1,0:T(8,128)(2,1)}, bf16[512,512]{1,0:T(8,128)(2,1)}, bf16[512,512]{1,0:T(8,128)(2,1)}) custom-call(bf16[512,512]{1,0:T(8,128)(2,1)S(1)} %copy-done, bf16[512,512]{1,0:T(8,128)(2,1)S(1)} %copy-done.1, bf16[512,512]{1,0:T(8,128)(2,1)S(1)} %copy-done.2, bf16[512,512]{1,0:T(8,128)(2,1)S(1)} %copy-done.3, ...), custom_call_target="tpu_custom_call" | custom-call | tf_op jit(solution)/shard_map/pallas_call | solution.py:368
  49.7 1.6 %collective-permute-done.4.refs_0_ = f32[16,128]{1,0:T(8,128)S(1)} collective-permute-done((f32[16,128]{1,0:T(8,128)S(1)}, f32[16,128]{1,0:T(8,128)S(1)}, u32[]{:S(2)}, u32[]{:S(2)}) %collective-permute-start.4) | collective-permute-done | bytes 8224 | tf_op jit(solution)/shard_map/ppermute | solution.py:307
  51.3 0.7 %shard_map.115 = (f32[8,16]{1,0:T(8,128)}, f32[1,16]{1,0:T(1,128)}) custom-call(f32[16,128]{1,0:T(8,128)S(1)} %collective-permute-done.4.refs_0_, f32[1,16]{1,0:T(1,128)S(1)} %bitcast.3), custom_call_target="tpu_custom_call" | custom-call | tf_op jit(solution)/shard_map/pallas_call | solution.py:376
  (5 shorter events, 0.0 us)
Async XLA Ops:
  0.6 18.3 %copy-start = (bf16[512,512]{1,0:T(8,128)(2,1)S(1)}, bf16[512,512]{1,0:T(8,128)(2,1)}, u32[]{:S(2)}) copy-start(bf16[512,512]{1,0:T(8,128)(2,1)} %key_ref.3) | copy-start | bytes 1572868
  0.6 18.3 %copy-start.1 = (bf16[512,512]{1,0:T(8,128)(2,1)S(1)}, bf16[512,512]{1,0:T(8,128)(2,1)}, u32[]{:S(2)}) copy-start(bf16[512,512]{1,0:T(8,128)(2,1)} %value_ref.3) | copy-start | bytes 1572868
  0.7 18.3 %copy-start.2 = (bf16[512,512]{1,0:T(8,128)(2,1)S(1)}, bf16[512,512]{1,0:T(8,128)(2,1)}, u32[]{:S(2)}) copy-start(bf16[512,512]{1,0:T(8,128)(2,1)} %query_ref.3) | copy-start | bytes 1572868
  0.7 18.3 %copy-start.3 = (bf16[512,512]{1,0:T(8,128)(2,1)S(1)}, bf16[512,512]{1,0:T(8,128)(2,1)}, u32[]{:S(2)}) copy-start(bf16[512,512]{1,0:T(8,128)(2,1)} %cot_ref.3) | copy-start | bytes 1572868
  1.9 17.0 %collective-permute-start = (bf16[128,512]{1,0:T(8,128)(2,1)S(1)}, bf16[128,512]{1,0:T(8,128)(2,1)S(1)}, u32[]{:S(2)}, u32[]{:S(2)}) collective-permute-start(bf16[128,512]{1,0:T(8,128)(2,1)S(1)} %get-tuple-element.20), channel_id=1, source_target_pairs={{0,16},{4,20},{8,24},{12,28},{16,32},{20,36},{24,40},{28,44},{32,4... | collective-permute-start | bytes 393224 | tf_op jit(solution)/shard_map/ppermute | solution.py:316
  3.8 16.9 %collective-permute-start.3 = (f32[8,128]{1,0:T(8,128)S(1)}, f32[8,128]{1,0:T(8,128)S(1)}, u32[]{:S(2)}, u32[]{:S(2)}) collective-permute-start(f32[8,128]{1,0:T(8,128)S(1)} %get-tuple-element.24), channel_id=1, source_target_pairs={{0,256},{1,320},{2,352},{3,288},{4,384},{5,448},{6,480},{7,416},{8... | collective-permute-start | bytes 12296 | tf_op jit(solution)/shard_map/ppermute | solution.py:307
  18.2 2.4 %collective-permute-start.1 = (bf16[128,512]{1,0:T(8,128)(2,1)S(1)}, bf16[128,512]{1,0:T(8,128)(2,1)S(1)}, u32[]{:S(2)}, u32[]{:S(2)}) collective-permute-start(bf16[128,512]{1,0:T(8,128)(2,1)S(1)} %get-tuple-element.21), channel_id=1, source_target_pairs={{1,17},{2,18},{3,19},{5,21},{6,22},{7,23},{9,25},{10,26},{11,27},{... | collective-permute-start | bytes 393224 | tf_op jit(solution)/shard_map/ppermute | solution.py:316
  21.4 14.7 %all-to-all-start = ((bf16[32,24,128]{2,1,0:T(8,128)(2,1)}), bf16[32,24,128]{2,1,0:T(8,128)(2,1)S(1)}, u32[]{:S(2)}, u32[]{:S(2)}) async-start(bf16[32,24,128]{2,1,0:T(8,128)(2,1)} %shard_map.112), calls=%async_computation | async-start | bytes 393216 | tf_op jit(solution)/shard_map/all_to_all | solution.py:361
  28.3 18.0 %collective-permute-start.2 = (bf16[128,512]{1,0:T(8,128)(2,1)S(1)}, bf16[128,512]{1,0:T(8,128)(2,1)S(1)}, u32[]{:S(2)}, u32[]{:S(2)}) collective-permute-start(bf16[128,512]{1,0:T(8,128)(2,1)S(1)} %get-tuple-element.22.head_ref), channel_id=1, source_target_pairs={{16,0},{17,1},{18,2},{19,3},{20,4},{21,5},{22,6},{23,7},{24,8},{25... | collective-permute-start | bytes 393224 | tf_op jit(solution)/shard_map/ppermute | solution.py:316
  36.4 14.9 %collective-permute-start.4 = (f32[16,128]{1,0:T(8,128)S(1)}, f32[16,128]{1,0:T(8,128)S(1)}, u32[]{:S(2)}, u32[]{:S(2)}) collective-permute-start(f32[16,128]{1,0:T(8,128)S(1)} %get-tuple-element.31), channel_id=1, source_target_pairs={{256,0},{320,1},{352,2},{288,3},{384,4},{448,5},{480,6},{416,7},{0... | collective-permute-start | bytes 24584 | tf_op jit(solution)/shard_map/ppermute | solution.py:307
  46.2 5.0 %copy-start.4 = (f32[16]{0:T(128)S(1)}, f32[16]{0:T(128)}, u32[]{:S(2)}) copy-start(f32[16]{0:T(128)} %param.11) | copy-start | bytes 196

commit v6 on v5

--- a/solution.py
+++ b/solution.py
@@ -28,13 +28,19 @@
     return (a.astype(F32) * b.astype(F32)).astype(BF16)
 
 
-def front_kernel(key, value, query, cot, weight, rate, tail_ref, late_tail_ref, taps_ref, *scratch):
+def front_kernel(key, value, query, cot, weight, rate, tail_ref, taps_ref, *scratch):
     refs, sems = scratch[:-1], scratch[-1]
     tail = pl.ds(key.shape[0] - FILT, FILT)
     sources = [weight, rate, key.at[tail], value.at[tail]]
     copies = [pltpu.make_async_copy(s, d, sems.at[i]) for i, (s, d) in enumerate(zip(sources, refs))]
-    for copy in copies:
+    for copy in copies[:2]:
         copy.start()
+
+    @pl.when(jnp.logical_not(is_late()))
+    def _():
+        for copy in copies[2:]:
+            copy.start()
+
     weight_ref, rate_ref = refs[:2]
     tap_count, group_count = weight.shape
     taps = (lax.axis_index("fsdp") * tap_count + iota((tap_count, group_count), 0)).astype(F32)
@@ -45,11 +51,16 @@
     high = decayed.astype(BF16).astype(F32)
     taps_ref[:, :group_count] = high
     taps_ref[:, group_count : 2 * group_count] = decayed - high
-    for copy in copies[2:]:
-        copy.wait()
-    products = rounded_product(refs[2][...], refs[3][...])
-    tail_ref[...] = products
-    late_tail_ref[...] = products
+
+    @pl.when(jnp.logical_not(is_late()))
+    def _():
+        for copy in copies[2:]:
+            copy.wait()
+        tail_ref[...] = rounded_product(refs[2][...], refs[3][...])
+
+
+def tail_kernel(key_ref, value_ref, tail_ref):
+    tail_ref[...] = rounded_product(key_ref[-FILT:], value_ref[-FILT:])
 
 
 LANDING = ((0, 2, 3, 1), (0, 1, 2, 3), (0, 1, 2, 3), (2, 0, 1, 3))
@@ -126,10 +137,30 @@
     @pl.when(is_late())
     def _():
         groups = LANES // GROUP
-        for tile in range(head_ref.shape[1] // LANES):
-            lanes = slice(tile * LANES, (tile + 1) * LANES)
-            rows = slice(tile * groups, (tile + 1) * groups)
-            total_ref[rows] = total_ref[rows] + diagonal_sums(head_ref[:, lanes], before_ref[:, lanes], LANES)
+        lane_group = (iota((FILT, 2 * LANES), 1) % LANES) // GROUP
+        zero = jnp.zeros((FILT, 2 * LANES), BF16)
+        same = iota((FILT, FILT), 0) >= iota((FILT, FILT), 1)
+        row = iota((2 * groups * 8, LANES), 0) % 8
+        for tile in range(0, head_ref.shape[1] // LANES, 2):
+            lanes = slice(tile * LANES, (tile + 2) * LANES)
+            head, before = head_ref[:, lanes], before_ref[:, lanes]
+            left = jnp.concatenate([jnp.where(lane_group == g, head, zero) for g in range(groups)], axis=0)
+            first = iota((FILT, 2 * LANES), 1) < LANES
+            right = jnp.concatenate([jnp.where(first, before, zero), jnp.where(first, zero, before)], axis=0)
+            outer = lax.dot_general(left, right, NT, preferred_element_type=F32)
+            total = jnp.zeros(row.shape, F32)
+            for i in range(0, FILT, 8):
+                parts = []
+                for side in range(2):
+                    for g in range(groups):
+                        part = outer[g * FILT + i : g * FILT + i + 8, side * FILT : (side + 1) * FILT]
+                        parts.append(jnp.where(same[i : i + 8], 0.0, part))
+                part = jnp.concatenate(parts, axis=0)
+                total = total + (pltpu.roll(part, FILT - i, axis=1) if i else part)
+            for step in (1, 2, 4):
+                total = jnp.where((row & step) != 0, pltpu.roll(total, FILT - step, axis=1), total)
+            rows = slice(tile * groups, (tile + 2) * groups)
+            total_ref[rows] = total_ref[rows] + total.reshape(2 * groups, 8, LANES).sum(axis=1)
 
     out_ref[...] = jnp.dot(total_ref[...].astype(BF16), flip_table(), preferred_element_type=F32)
 
@@ -327,10 +358,10 @@
 
     edge = (FILT, channels)
     anywhere = pl.BlockSpec(memory_space=pl.ANY)
-    tail, late_tail, taps = pl.pallas_call(
+    tail, taps = pl.pallas_call(
         front_kernel,
         in_specs=[anywhere] * 6,
-        out_shape=[sds(edge, BF16)] * 2 + [sds((tap_count, LANES), F32)],
+        out_shape=[sds(edge, BF16)] + [sds((tap_count, LANES), F32)],
         scratch_shapes=[pltpu.VMEM(filter_weight.shape, F32), pltpu.VMEM(rate_row.shape, F32)]
         + [pltpu.VMEM(edge, BF16)] * 2
         + [pltpu.SemaphoreType.DMA((4,))],
@@ -338,6 +369,9 @@
     )(*(in_hbm(x) for x in (key_in, value_in, query, cotangent, filter_weight, rate_row)))
     taps_here = moved_pieces(taps, False)
     early = passed_along(tail, 1, lambda f: f % SIDE == 0)
+    late_tail = pl.pallas_call(
+        tail_kernel, out_shape=sds(edge, BF16), compiler_params=params()
+    )(key_in, value_in)
     late = passed_along(late_tail, 1, lambda f: f % SIDE != 0)
 
     sums, head = pl.pallas_call(

time: 52.2 us -> 52.1 us (level)
  transfers between devices with their start and end apart: 6 -> 6, of which waited for: 2 -> 2; matrix products, arithmetic and copies ran while one was open for 0% -> 0% of each run, Pallas kernels for 10% -> 11%
where the time goes in v6:
time: 52.1 us; the launch traced here: 51.8 us
  starting transfers between devices  35.7 us (69%)
  Pallas kernels  7.99 us (15%)
  waiting for transfers between devices  7.26 us (14%)
  between operations  0.81 us (2%)
    ppermute x2, starting transfers between devices, moved_pieces(): lax.ppermute(value, ('ctx', 'fsdp'), [(b, a) for a, b in pairs] if back e...  24.1 us
    all_to_all x1, starting transfers between devices, per_device(): received = lax.all_to_all(message, 'ctx', 0, 0, tiled=True)  6.81 us
    all_to_all x1, waiting for transfers between devices, per_device(): received = lax.all_to_all(message, 'ctx', 0, 0, tiled=True)  5.65 us
    ppermute x3, starting transfers between devices, passed_along(): return lax.ppermute(value, ('ctx', 'fsdp'), pairs)  4.81 us
    pallas_call x1, Pallas kernels, per_device(): pl.pallas_call(outputs_kernel, out_specs=[anywhere] * 4, out_shape=[sds((...  3.45 us
    pallas_call x1, Pallas kernels, per_device(): pl.pallas_call(sums_kernel, out_shape=[sds((groups, LANES), F32), sds(edg...  1.62 us
    ppermute x2, waiting for transfers between devices, moved_pieces(): lax.ppermute(value, ('ctx', 'fsdp'), [(b, a) for a, b in pairs] if back e...  1.6 us
    pallas_call x1, Pallas kernels, per_device(): pl.pallas_call(front_kernel, in_specs=[anywhere] * 6, out_shape=[sds(edge...  1.15 us
  transfers between devices with their start and end apart: 6, of which 2 were waited for; matrix products, arithmetic and copies ran while one was open for 0% of the time, Pallas kernels for 11%

profile of v6, /device:TPU:64, one launch (start us, length us, event | category | flops | bytes accessed | tf_op | source)
XLA Modules:
  0.0 51.8 jit_solution(3790307149417835825)
XLA Ops:
  0.6 0.0 copy-start
  0.6 0.0 copy-start.1
  0.7 1.2 %shard_map.109 = (bf16[128,512]{1,0:T(8,128)(2,1)S(1)}, f32[8,128]{1,0:T(8,128)S(1)}) custom-call(bf16[512,512]{1,0:T(8,128)(2,1)} %key_ref.5, bf16[512,512]{1,0:T(8,128)(2,1)} %value_ref.5, bf16[512,512]{1,0:T(8,128)(2,1)} %query_ref.3, bf16[512,512]{1,0:T(8,128)(2,1)} %cot_ref.3, f32[8,16]{1,0:T(8,128)} %weight.1, f32[1,16]{1,0:T(1,128)} %bitcast.2), custom_call_target="tpu_custom_call" | custom-call | tf_op jit(solution)/shard_map/pallas_call | solution.py:361
  1.8 1.9 %collective-permute-start = (bf16[128,512]{1,0:T(8,128)(2,1)S(1)}, bf16[128,512]{1,0:T(8,128)(2,1)S(1)}, u32[]{:S(2)}, u32[]{:S(2)}) collective-permute-start(bf16[128,512]{1,0:T(8,128)(2,1)S(1)} %get-tuple-element.19), channel_id=1, source_target_pairs={{0,16},{4,20},{8,24},{12,28},{16,32},{20,36},{24,40},{28,44},{32,4... | collective-permute-start | bytes 393224 | tf_op jit(solution)/shard_map/ppermute | solution.py:347
  3.7 0.0 copy-start.2
  3.8 0.0 copy-start.3
  3.8 14.3 %collective-permute-start.3 = (f32[8,128]{1,0:T(8,128)S(1)}, f32[8,128]{1,0:T(8,128)S(1)}, u32[]{:S(2)}, u32[]{:S(2)}) collective-permute-start(f32[8,128]{1,0:T(8,128)S(1)} %get-tuple-element.22), channel_id=1, source_target_pairs={{0,256},{1,320},{2,352},{3,288},{4,384},{5,448},{6,480},{7,416},{8... | collective-permute-start | bytes 12296 | tf_op jit(solution)/shard_map/ppermute | solution.py:338
  18.1 0.7 %collective-permute-start.1 = (bf16[128,512]{1,0:T(8,128)(2,1)S(1)}, bf16[128,512]{1,0:T(8,128)(2,1)S(1)}, u32[]{:S(2)}, u32[]{:S(2)}) collective-permute-start(bf16[128,512]{1,0:T(8,128)(2,1)S(1)} %shard_map.110), channel_id=1, source_target_pairs={{1,17},{2,18},{3,19},{5,21},{6,22},{7,23},{9,25},{10,26},{11,27},{... | collective-permute-start | bytes 393224 | tf_op jit(solution)/shard_map/ppermute | solution.py:347
  18.8 0.0 collective-permute-done.before_ref.early_ref
  18.8 1.6 %shard_map.111 = (f32[32,128]{1,0:T(8,128)S(1)}, bf16[128,512]{1,0:T(8,128)(2,1)S(1)}) custom-call(bf16[512,512]{1,0:T(8,128)(2,1)S(1)} %copy-done, bf16[512,512]{1,0:T(8,128)(2,1)S(1)} %copy-done.1, bf16[512,512]{1,0:T(8,128)(2,1)S(1)} %copy-done.2, bf16[512,512]{1,0:T(8,128)(2,1)S(1)} %copy-done.3, ...), custom_call_target="tpu_custom_call" | custom-call | flops 3000000000 | bytes 9000000 | tf_op jit(solution)/shard_map/pallas_call | solution.py:377
  20.4 0.0 collective-permute-done.1.before_ref.late_ref
  20.5 0.1 shard_map.112.sums_ref
  20.6 0.0 collective-permute-done.3.taps_ref
  20.6 0.7 %shard_map.113 = bf16[32,24,128]{2,1,0:T(8,128)(2,1)} custom-call(f32[32,128]{1,0:T(8,128)S(1)} %shard_map.112.sums_ref, f32[8,128]{1,0:T(8,128)S(1)} %collective-permute-done.3.taps_ref), custom_call_target="tpu_custom_call" | custom-call | tf_op jit(solution)/shard_map/pallas_call | solution.py:390
  21.3 6.8 %all-to-all-start = ((bf16[32,24,128]{2,1,0:T(8,128)(2,1)}), bf16[32,24,128]{2,1,0:T(8,128)(2,1)S(1)}, u32[]{:S(2)}, u32[]{:S(2)}) async-start(bf16[32,24,128]{2,1,0:T(8,128)(2,1)} %shard_map.113), calls=%async_computation | async-start | bytes 393216 | tf_op jit(solution)/shard_map/all_to_all | solution.py:395
  28.1 2.2 %collective-permute-start.2 = (bf16[128,512]{1,0:T(8,128)(2,1)S(1)}, bf16[128,512]{1,0:T(8,128)(2,1)S(1)}, u32[]{:S(2)}, u32[]{:S(2)}) collective-permute-start(bf16[128,512]{1,0:T(8,128)(2,1)S(1)} %get-tuple-element.20.head_ref), channel_id=1, source_target_pairs={{16,0},{17,1},{18,2},{19,3},{20,4},{21,5},{22,6},{23,7},{24,8},{25... | collective-permute-start | bytes 393224 | tf_op jit(solution)/shard_map/ppermute | solution.py:347
  30.4 5.6 %all-to-all-done.recv_ref = bf16[32,24,128]{2,1,0:T(8,128)(2,1)S(1)} async-done(((bf16[32,24,128]{2,1,0:T(8,128)(2,1)}), bf16[32,24,128]{2,1,0:T(8,128)(2,1)S(1)}, u32[]{:S(2)}, u32[]{:S(2)}) %all-to-all-start) | async-done | bytes 196640 | tf_op jit(solution)/shard_map/all_to_all | solution.py:395
  36.0 0.2 shard_map.114
  36.2 9.8 %collective-permute-start.4 = (f32[16,128]{1,0:T(8,128)S(1)}, f32[16,128]{1,0:T(8,128)S(1)}, u32[]{:S(2)}, u32[]{:S(2)}) collective-permute-start(f32[16,128]{1,0:T(8,128)S(1)} %get-tuple-element.29), channel_id=1, source_target_pairs={{256,0},{320,1},{352,2},{288,3},{384,4},{448,5},{480,6},{416,7},{0... | collective-permute-start | bytes 24584 | tf_op jit(solution)/shard_map/ppermute | solution.py:338
  46.1 0.0 collective-permute-done.2.after_ref
  46.1 0.0 copy-start.4
  46.1 3.5 %shard_map.115 = (bf16[512,512]{1,0:T(8,128)(2,1)}, bf16[512,512]{1,0:T(8,128)(2,1)}, bf16[512,512]{1,0:T(8,128)(2,1)}, bf16[512,512]{1,0:T(8,128)(2,1)}) custom-call(bf16[512,512]{1,0:T(8,128)(2,1)S(1)} %copy-done, bf16[512,512]{1,0:T(8,128)(2,1)S(1)} %copy-done.1, bf16[512,512]{1,0:T(8,128)(2,1)S(1)} %copy-done.2, bf16[512,512]{1,0:T(8,128)(2,1)S(1)} %copy-done.3, ...), custom_call_target="tpu_custom_call" | custom-call | tf_op jit(solution)/shard_map/pallas_call | solution.py:402
  49.5 1.6 %collective-permute-done.4.refs_0_ = f32[16,128]{1,0:T(8,128)S(1)} collective-permute-done((f32[16,128]{1,0:T(8,128)S(1)}, f32[16,128]{1,0:T(8,128)S(1)}, u32[]{:S(2)}, u32[]{:S(2)}) %collective-permute-start.4) | collective-permute-done | bytes 8224 | tf_op jit(solution)/shard_map/ppermute | solution.py:338
  51.1 0.7 %shard_map.116 = (f32[8,16]{1,0:T(8,128)}, f32[1,16]{1,0:T(1,128)}) custom-call(f32[16,128]{1,0:T(8,128)S(1)} %collective-permute-done.4.refs_0_, f32[1,16]{1,0:T(1,128)S(1)} %bitcast.3), custom_call_target="tpu_custom_call" | custom-call | tf_op jit(solution)/shard_map/pallas_call | solution.py:410
  (6 shorter events, 0.0 us)
Async XLA Ops:
  0.6 17.4 %copy-start = (bf16[512,512]{1,0:T(8,128)(2,1)S(1)}, bf16[512,512]{1,0:T(8,128)(2,1)}, u32[]{:S(2)}) copy-start(bf16[512,512]{1,0:T(8,128)(2,1)} %key_ref.5) | copy-start | bytes 1572868
  0.6 17.4 %copy-start.1 = (bf16[512,512]{1,0:T(8,128)(2,1)S(1)}, bf16[512,512]{1,0:T(8,128)(2,1)}, u32[]{:S(2)}) copy-start(bf16[512,512]{1,0:T(8,128)(2,1)} %value_ref.5) | copy-start | bytes 1572868
  1.8 17.0 %collective-permute-start = (bf16[128,512]{1,0:T(8,128)(2,1)S(1)}, bf16[128,512]{1,0:T(8,128)(2,1)S(1)}, u32[]{:S(2)}, u32[]{:S(2)}) collective-permute-start(bf16[128,512]{1,0:T(8,128)(2,1)S(1)} %get-tuple-element.19), channel_id=1, source_target_pairs={{0,16},{4,20},{8,24},{12,28},{16,32},{20,36},{24,40},{28,44},{32,4... | collective-permute-start | bytes 393224 | tf_op jit(solution)/shard_map/ppermute | solution.py:347
  3.7 15.1 %copy-start.2 = (bf16[512,512]{1,0:T(8,128)(2,1)S(1)}, bf16[512,512]{1,0:T(8,128)(2,1)}, u32[]{:S(2)}) copy-start(bf16[512,512]{1,0:T(8,128)(2,1)} %query_ref.3) | copy-start | bytes 1572868
  3.8 15.1 %copy-start.3 = (bf16[512,512]{1,0:T(8,128)(2,1)S(1)}, bf16[512,512]{1,0:T(8,128)(2,1)}, u32[]{:S(2)}) copy-start(bf16[512,512]{1,0:T(8,128)(2,1)} %cot_ref.3) | copy-start | bytes 1572868
  3.8 16.8 %collective-permute-start.3 = (f32[8,128]{1,0:T(8,128)S(1)}, f32[8,128]{1,0:T(8,128)S(1)}, u32[]{:S(2)}, u32[]{:S(2)}) collective-permute-start(f32[8,128]{1,0:T(8,128)S(1)} %get-tuple-element.22), channel_id=1, source_target_pairs={{0,256},{1,320},{2,352},{3,288},{4,384},{5,448},{6,480},{7,416},{8... | collective-permute-start | bytes 12296 | tf_op jit(solution)/shard_map/ppermute | solution.py:338
  18.1 2.3 %collective-permute-start.1 = (bf16[128,512]{1,0:T(8,128)(2,1)S(1)}, bf16[128,512]{1,0:T(8,128)(2,1)S(1)}, u32[]{:S(2)}, u32[]{:S(2)}) collective-permute-start(bf16[128,512]{1,0:T(8,128)(2,1)S(1)} %shard_map.110), channel_id=1, source_target_pairs={{1,17},{2,18},{3,19},{5,21},{6,22},{7,23},{9,25},{10,26},{11,27},{... | collective-permute-start | bytes 393224 | tf_op jit(solution)/shard_map/ppermute | solution.py:347
  21.3 14.7 %all-to-all-start = ((bf16[32,24,128]{2,1,0:T(8,128)(2,1)}), bf16[32,24,128]{2,1,0:T(8,128)(2,1)S(1)}, u32[]{:S(2)}, u32[]{:S(2)}) async-start(bf16[32,24,128]{2,1,0:T(8,128)(2,1)} %shard_map.113), calls=%async_computation | async-start | bytes 393216 | tf_op jit(solution)/shard_map/all_to_all | solution.py:395
  28.1 17.9 %collective-permute-start.2 = (bf16[128,512]{1,0:T(8,128)(2,1)S(1)}, bf16[128,512]{1,0:T(8,128)(2,1)S(1)}, u32[]{:S(2)}, u32[]{:S(2)}) collective-permute-start(bf16[128,512]{1,0:T(8,128)(2,1)S(1)} %get-tuple-element.20.head_ref), channel_id=1, source_target_pairs={{16,0},{17,1},{18,2},{19,3},{20,4},{21,5},{22,6},{23,7},{24,8},{25... | collective-permute-start | bytes 393224 | tf_op jit(solution)/shard_map/ppermute | solution.py:347
  36.2 14.9 %collective-permute-start.4 = (f32[16,128]{1,0:T(8,128)S(1)}, f32[16,128]{1,0:T(8,128)S(1)}, u32[]{:S(2)}, u32[]{:S(2)}) collective-permute-start(f32[16,128]{1,0:T(8,128)S(1)} %get-tuple-element.29), channel_id=1, source_target_pairs={{256,0},{320,1},{352,2},{288,3},{384,4},{448,5},{480,6},{416,7},{0... | collective-permute-start | bytes 24584 | tf_op jit(solution)/shard_map/ppermute | solution.py:338
  46.1 5.1 %copy-start.4 = (f32[16]{0:T(128)S(1)}, f32[16]{0:T(128)}, u32[]{:S(2)}) copy-start(f32[16]{0:T(128)} %param.11) | copy-start | bytes 196

commit v7 on v6

--- a/solution.py
+++ b/solution.py
@@ -63,7 +63,7 @@
     tail_ref[...] = rounded_product(key_ref[-FILT:], value_ref[-FILT:])
 
 
-LANDING = ((0, 2, 3, 1), (0, 1, 2, 3), (0, 1, 2, 3), (2, 0, 1, 3))
+LANDING = ((1, 2, 3, 0), (0, 1, 2, 3), (0, 1, 2, 3), (2, 0, 1, 3))
 SIDE = 4
 
 

time: 52.1 us -> 52.7 us (1.012)
  the two profiles are of different devices: /device:TPU:64 before, /device:TPU:1 now
where the time goes in v7:
time: 52.7 us; the launch traced here: 52.4 us
  starting transfers between devices  32.3 us (61%)
  waiting for transfers between devices  11.2 us (21%)
  Pallas kernels  7.98 us (15%)
  between operations  0.82 us (2%)
    ppermute x2, starting transfers between devices, moved_pieces(): lax.ppermute(value, ('ctx', 'fsdp'), [(b, a) for a, b in pairs] if back e...  14.4 us
    all_to_all x1, starting transfers between devices, per_device(): received = lax.all_to_all(message, 'ctx', 0, 0, tiled=True)  10.2 us
    all_to_all x1, waiting for transfers between devices, per_device(): received = lax.all_to_all(message, 'ctx', 0, 0, tiled=True)  7.76 us
    ppermute x3, starting transfers between devices, passed_along(): return lax.ppermute(value, ('ctx', 'fsdp'), pairs)  7.75 us
    ppermute x2, waiting for transfers between devices, moved_pieces(): lax.ppermute(value, ('ctx', 'fsdp'), [(b, a) for a, b in pairs] if back e...  3.47 us
    pallas_call x1, Pallas kernels, per_device(): pl.pallas_call(outputs_kernel, out_specs=[anywhere] * 4, out_shape=[sds((...  3.45 us
    pallas_call x1, Pallas kernels, per_device(): pl.pallas_call(sums_kernel, out_shape=[sds((groups, LANES), F32), sds(edg...  1.62 us
    pallas_call x1, Pallas kernels, per_device(): pl.pallas_call(front_kernel, in_specs=[anywhere] * 6, out_shape=[sds(edge...  1.15 us
  transfers between devices with their start and end apart: 6, of which 2 were waited for; matrix products, arithmetic and copies ran while one was open for 0% of the time, Pallas kernels for 10%

profile of v7, /device:TPU:1, one launch (start us, length us, event | category | flops | bytes accessed | tf_op | source)
XLA Modules:
  0.0 52.4 jit_solution(16641535328634196273)
XLA Ops:
  0.7 1.2 %shard_map.109 = (bf16[128,512]{1,0:T(8,128)(2,1)S(1)}, f32[8,128]{1,0:T(8,128)S(1)}) custom-call(bf16[512,512]{1,0:T(8,128)(2,1)} %key_ref.5, bf16[512,512]{1,0:T(8,128)(2,1)} %value_ref.5, bf16[512,512]{1,0:T(8,128)(2,1)} %query_ref.3, bf16[512,512]{1,0:T(8,128)(2,1)} %cot_ref.3, f32[8,16]{1,0:T(8,128)} %weight.1, f32[1,16]{1,0:T(1,128)} %bitcast.2), custom_call_target="tpu_custom_call" | custom-call | tf_op jit(solution)/shard_map/pallas_call | solution.py:361
  1.8 4.9 %collective-permute-start = (bf16[128,512]{1,0:T(8,128)(2,1)S(1)}, bf16[128,512]{1,0:T(8,128)(2,1)S(1)}, u32[]{:S(2)}, u32[]{:S(2)}) collective-permute-start(bf16[128,512]{1,0:T(8,128)(2,1)S(1)} %get-tuple-element.19), channel_id=1, source_target_pairs={{0,16},{4,20},{8,24},{12,28},{16,32},{20,36},{24,40},{28,44},{32,4... | collective-permute-start | bytes 393224 | tf_op jit(solution)/shard_map/ppermute | solution.py:347
  6.8 0.0 copy-start.2
  6.8 0.0 copy-start.3
  6.8 6.3 %collective-permute-start.3 = (f32[8,128]{1,0:T(8,128)S(1)}, f32[8,128]{1,0:T(8,128)S(1)}, u32[]{:S(2)}, u32[]{:S(2)}) collective-permute-start(f32[8,128]{1,0:T(8,128)S(1)} %get-tuple-element.22), channel_id=1, source_target_pairs={{0,288},{1,320},{2,352},{3,256},{4,416},{5,448},{6,480},{7,384},{8... | collective-permute-start | bytes 12296 | tf_op jit(solution)/shard_map/ppermute | solution.py:338
  13.1 0.0 copy-done
  13.1 0.0 copy-done.1
  13.2 0.7 %collective-permute-start.1 = (bf16[128,512]{1,0:T(8,128)(2,1)S(1)}, bf16[128,512]{1,0:T(8,128)(2,1)S(1)}, u32[]{:S(2)}, u32[]{:S(2)}) collective-permute-start(bf16[128,512]{1,0:T(8,128)(2,1)S(1)} %shard_map.110), channel_id=1, source_target_pairs={{1,17},{2,18},{3,19},{5,21},{6,22},{7,23},{9,25},{10,26},{11,27},{... | collective-permute-start | bytes 393224 | tf_op jit(solution)/shard_map/ppermute | solution.py:347
  13.8 0.0 collective-permute-done.before_ref.early_ref
  13.9 1.6 %shard_map.111 = (f32[32,128]{1,0:T(8,128)S(1)}, bf16[128,512]{1,0:T(8,128)(2,1)S(1)}) custom-call(bf16[512,512]{1,0:T(8,128)(2,1)S(1)} %copy-done, bf16[512,512]{1,0:T(8,128)(2,1)S(1)} %copy-done.1, bf16[512,512]{1,0:T(8,128)(2,1)S(1)} %copy-done.2, bf16[512,512]{1,0:T(8,128)(2,1)S(1)} %copy-done.3, ...), custom_call_target="tpu_custom_call" | custom-call | flops 3000000000 | bytes 9000000 | tf_op jit(solution)/shard_map/pallas_call | solution.py:377
  15.5 0.0 collective-permute-done.1.before_ref.late_ref
  15.5 0.1 shard_map.112.sums_ref
  15.7 3.5 %collective-permute-done.3.taps_ref = f32[8,128]{1,0:T(8,128)S(1)} collective-permute-done((f32[8,128]{1,0:T(8,128)S(1)}, f32[8,128]{1,0:T(8,128)S(1)}, u32[]{:S(2)}, u32[]{:S(2)}) %collective-permute-start.3) | collective-permute-done | bytes 4128 | tf_op jit(solution)/shard_map/ppermute | solution.py:338
  19.1 0.7 %shard_map.113 = bf16[32,24,128]{2,1,0:T(8,128)(2,1)} custom-call(f32[32,128]{1,0:T(8,128)S(1)} %shard_map.112.sums_ref, f32[8,128]{1,0:T(8,128)S(1)} %collective-permute-done.3.taps_ref), custom_call_target="tpu_custom_call" | custom-call | tf_op jit(solution)/shard_map/pallas_call | solution.py:390
  19.8 10.2 %all-to-all-start = ((bf16[32,24,128]{2,1,0:T(8,128)(2,1)}), bf16[32,24,128]{2,1,0:T(8,128)(2,1)S(1)}, u32[]{:S(2)}, u32[]{:S(2)}) async-start(bf16[32,24,128]{2,1,0:T(8,128)(2,1)} %shard_map.113), calls=%async_computation | async-start | bytes 393216 | tf_op jit(solution)/shard_map/all_to_all | solution.py:395
  30.0 2.1 %collective-permute-start.2 = (bf16[128,512]{1,0:T(8,128)(2,1)S(1)}, bf16[128,512]{1,0:T(8,128)(2,1)S(1)}, u32[]{:S(2)}, u32[]{:S(2)}) collective-permute-start(bf16[128,512]{1,0:T(8,128)(2,1)S(1)} %get-tuple-element.20.head_ref), channel_id=1, source_target_pairs={{16,0},{17,1},{18,2},{19,3},{20,4},{21,5},{22,6},{23,7},{24,8},{25... | collective-permute-start | bytes 393224 | tf_op jit(solution)/shard_map/ppermute | solution.py:347
  32.1 7.8 %all-to-all-done.recv_ref = bf16[32,24,128]{2,1,0:T(8,128)(2,1)S(1)} async-done(((bf16[32,24,128]{2,1,0:T(8,128)(2,1)}), bf16[32,24,128]{2,1,0:T(8,128)(2,1)S(1)}, u32[]{:S(2)}, u32[]{:S(2)}) %all-to-all-start) | async-done | bytes 196640 | tf_op jit(solution)/shard_map/all_to_all | solution.py:395
  39.9 0.2 shard_map.114
  40.1 8.1 %collective-permute-start.4 = (f32[16,128]{1,0:T(8,128)S(1)}, f32[16,128]{1,0:T(8,128)S(1)}, u32[]{:S(2)}, u32[]{:S(2)}) collective-permute-start(f32[16,128]{1,0:T(8,128)S(1)} %get-tuple-element.29), channel_id=1, source_target_pairs={{288,0},{320,1},{352,2},{256,3},{416,4},{448,5},{480,6},{384,7},{3... | collective-permute-start | bytes 24584 | tf_op jit(solution)/shard_map/ppermute | solution.py:338
  48.2 0.0 collective-permute-done.2.after_ref
  48.3 0.0 copy-start.4
  48.3 3.5 %shard_map.115 = (bf16[512,512]{1,0:T(8,128)(2,1)}, bf16[512,512]{1,0:T(8,128)(2,1)}, bf16[512,512]{1,0:T(8,128)(2,1)}, bf16[512,512]{1,0:T(8,128)(2,1)}) custom-call(bf16[512,512]{1,0:T(8,128)(2,1)S(1)} %copy-done, bf16[512,512]{1,0:T(8,128)(2,1)S(1)} %copy-done.1, bf16[512,512]{1,0:T(8,128)(2,1)S(1)} %copy-done.2, bf16[512,512]{1,0:T(8,128)(2,1)S(1)} %copy-done.3, ...), custom_call_target="tpu_custom_call" | custom-call | tf_op jit(solution)/shard_map/pallas_call | solution.py:402
  51.7 0.0 collective-permute-done.4.refs_0_
  51.8 0.7 %shard_map.116 = (f32[8,16]{1,0:T(8,128)}, f32[1,16]{1,0:T(1,128)}) custom-call(f32[16,128]{1,0:T(8,128)S(1)} %collective-permute-done.4.refs_0_, f32[1,16]{1,0:T(1,128)S(1)} %bitcast.3), custom_call_target="tpu_custom_call" | custom-call | tf_op jit(solution)/shard_map/pallas_call | solution.py:410
  (6 shorter events, 0.0 us)
Async XLA Ops:
  0.6 12.5 %copy-start = (bf16[512,512]{1,0:T(8,128)(2,1)S(1)}, bf16[512,512]{1,0:T(8,128)(2,1)}, u32[]{:S(2)}) copy-start(bf16[512,512]{1,0:T(8,128)(2,1)} %key_ref.5) | copy-start | bytes 1572868
  0.6 12.5 %copy-start.1 = (bf16[512,512]{1,0:T(8,128)(2,1)S(1)}, bf16[512,512]{1,0:T(8,128)(2,1)}, u32[]{:S(2)}) copy-start(bf16[512,512]{1,0:T(8,128)(2,1)} %value_ref.5) | copy-start | bytes 1572868
  1.8 12.0 %collective-permute-start = (bf16[128,512]{1,0:T(8,128)(2,1)S(1)}, bf16[128,512]{1,0:T(8,128)(2,1)S(1)}, u32[]{:S(2)}, u32[]{:S(2)}) collective-permute-start(bf16[128,512]{1,0:T(8,128)(2,1)S(1)} %get-tuple-element.19), channel_id=1, source_target_pairs={{0,16},{4,20},{8,24},{12,28},{16,32},{20,36},{24,40},{28,44},{32,4... | collective-permute-start | bytes 393224 | tf_op jit(solution)/shard_map/ppermute | solution.py:347
  6.8 7.1 %copy-start.2 = (bf16[512,512]{1,0:T(8,128)(2,1)S(1)}, bf16[512,512]{1,0:T(8,128)(2,1)}, u32[]{:S(2)}) copy-start(bf16[512,512]{1,0:T(8,128)(2,1)} %query_ref.3) | copy-start | bytes 1572868
  6.8 7.1 %copy-start.3 = (bf16[512,512]{1,0:T(8,128)(2,1)S(1)}, bf16[512,512]{1,0:T(8,128)(2,1)}, u32[]{:S(2)}) copy-start(bf16[512,512]{1,0:T(8,128)(2,1)} %cot_ref.3) | copy-start | bytes 1572868
  6.8 12.3 %collective-permute-start.3 = (f32[8,128]{1,0:T(8,128)S(1)}, f32[8,128]{1,0:T(8,128)S(1)}, u32[]{:S(2)}, u32[]{:S(2)}) collective-permute-start(f32[8,128]{1,0:T(8,128)S(1)} %get-tuple-element.22), channel_id=1, source_target_pairs={{0,288},{1,320},{2,352},{3,256},{4,416},{5,448},{6,480},{7,384},{8... | collective-permute-start | bytes 12296 | tf_op jit(solution)/shard_map/ppermute | solution.py:338
  13.2 2.3 %collective-permute-start.1 = (bf16[128,512]{1,0:T(8,128)(2,1)S(1)}, bf16[128,512]{1,0:T(8,128)(2,1)S(1)}, u32[]{:S(2)}, u32[]{:S(2)}) collective-permute-start(bf16[128,512]{1,0:T(8,128)(2,1)S(1)} %shard_map.110), channel_id=1, source_target_pairs={{1,17},{2,18},{3,19},{5,21},{6,22},{7,23},{9,25},{10,26},{11,27},{... | collective-permute-start | bytes 393224 | tf_op jit(solution)/shard_map/ppermute | solution.py:347
  19.8 20.1 %all-to-all-start = ((bf16[32,24,128]{2,1,0:T(8,128)(2,1)}), bf16[32,24,128]{2,1,0:T(8,128)(2,1)S(1)}, u32[]{:S(2)}, u32[]{:S(2)}) async-start(bf16[32,24,128]{2,1,0:T(8,128)(2,1)} %shard_map.113), calls=%async_computation | async-start | bytes 393216 | tf_op jit(solution)/shard_map/all_to_all | solution.py:395
  30.0 18.3 %collective-permute-start.2 = (bf16[128,512]{1,0:T(8,128)(2,1)S(1)}, bf16[128,512]{1,0:T(8,128)(2,1)S(1)}, u32[]{:S(2)}, u32[]{:S(2)}) collective-permute-start(bf16[128,512]{1,0:T(8,128)(2,1)S(1)} %get-tuple-element.20.head_ref), channel_id=1, source_target_pairs={{16,0},{17,1},{18,2},{19,3},{20,4},{21,5},{22,6},{23,7},{24,8},{25... | collective-permute-start | bytes 393224 | tf_op jit(solution)/shard_map/ppermute | solution.py:347
  40.1 11.6 %collective-permute-start.4 = (f32[16,128]{1,0:T(8,128)S(1)}, f32[16,128]{1,0:T(8,128)S(1)}, u32[]{:S(2)}, u32[]{:S(2)}) collective-permute-start(f32[16,128]{1,0:T(8,128)S(1)} %get-tuple-element.29), channel_id=1, source_target_pairs={{288,0},{320,1},{352,2},{256,3},{416,4},{448,5},{480,6},{384,7},{3... | collective-permute-start | bytes 24584 | tf_op jit(solution)/shard_map/ppermute | solution.py:338
  48.3 3.5 %copy-start.4 = (f32[16]{0:T(128)S(1)}, f32[16]{0:T(128)}, u32[]{:S(2)}) copy-start(f32[16]{0:T(128)} %param.11) | copy-start | bytes 196
